TPU v7x, 32 devices: a whole 2x2x4 slice. The times are simulated.
32 devices in a mesh: region: 8 (over z, y), scen: 4 (over x, core).
Axes of the slice: x: 2, y: 2, z: 4, core: 2. Of those that a mesh axis runs over, the one named last changes fastest.
Arguments:
- inverse_blocks: float32 [256, 5, 96, 96], P('region')
- block_cols: int32 [256, 5], P('region'), may hold values from 0 to 31, as said below
- source_current: float32 [24576], P('region'), may hold values from -6 to 6
- node_decay: float32 [24576], P('region'), may hold values from 0.3 to 0.95
- node_gain: float32 [24576], P('region'), may hold values from 0.05 to 0.5
- voltage_init: float32 [256, 24576], P('scen', 'region'), may hold values from -6 to 6
- branch_init: float32 [256, 24576], P('scen', 'region'), may hold values from -3 to 3
- wave_init: float32 [8, 256, 2048], P(None, 'scen', 'region'), may hold values from -6 to 6
- line_node: int32 [2048], P('region'), may hold values from 0 to 3071
- line_delay: int32 [2048], P('region'), may hold values from 1 to 8, as said below
- line_admittance: float32 [2048], P('region'), may hold values from 0.19 to 1, as said below
- conv_region: int32 [3072, 1], P('region'), may hold values from 0 to 7; in each aligned block of 384 rows (0 to 383, 384 to 767, ...) at most 115 rows name the same one
- conv_node: int32 [3072], P('region'), may hold values from 0 to 3071
- conv_power: float32 [3072], P('region'), may hold values from 0.3 to 3
- conv_gains: float32 [2, 3072], P(None, 'region'), may hold values from 0.2 to 0.9
- conv_init: float32 [2, 256, 3072], P(None, 'scen', 'region'), may hold values from -3 to 3
- fault_node: int32 [256], P('scen'), may hold values from 0 to 24575
- fault_kind: int32 [256], P('scen'), may hold values from 0 to 3
Outputs:
- voltage: float32 [256, 24576], P('scen', 'region')
- branch_history: float32 [256, 24576], P('scen', 'region')
- wave_history: float32 [8, 256, 2048], P(None, 'scen', 'region')
- conv_state: float32 [2, 256, 3072], P(None, 'scen', 'region')
- envelope: float32 [24576], P('region')
Inputs may be any that keep to these rules, and one draw needn't show every extreme that they name: `block_cols`: entry 0 of row b is b mod 32; the 5 entries of a row are distinct. `line_delay`: entry r * 2 * 128 + l with l < 128 equals entry ((r - 1) mod 8) * 2 * 128 + 128 + l: both ends of a line have one delay. `line_admittance`: entry r * 2 * 128 + l with l < 128 equals entry ((r - 1) mod 8) * 2 * 128 + 128 + l: both ends of a line have one admittance. `conv_region`: among the converters of one region index of the mesh (aligned blocks of 384 rows), at most 115 lie in one region, and some region gets exactly 115.
All inputs are finite; a program needn't handle non-finite values.
Results may differ from a plain program's by a relative error of at most 0.00011.
Values sent between devices are 32-bit elements; how exact they have to be, the bound alone decides.
No kernel may reach another device: no remote copies, remote signals or barrier semaphores. Data moves between devices by JAX's collectives and lax.ppermute only.
A program may use at most 128 MiB of HBM per device.

v0:
```python
import functools
import math

import jax
import jax.numpy as jnp
from jax import lax
from jax.experimental import pallas as pl
from jax.experimental.pallas import tpu as pltpu
from jax.sharding import PartitionSpec as P

STEPS = 4
LANES = 128
BF = jnp.bfloat16
F32 = jnp.float32
I32 = jnp.int32
VMEM = pl.BlockSpec(memory_space=pltpu.VMEM)
SMEM = pl.BlockSpec(memory_space=pltpu.SMEM)
HBM = pl.BlockSpec(memory_space=pltpu.HBM)


def round_up(value, unit):
    return -(-value // unit) * unit


def iota(shape, dim):
    return lax.broadcasted_iota(I32, shape, dim)


def split_2(value):
    high = value.astype(BF)
    return high, (value - high.astype(F32)).astype(BF)


def split_3(value):
    high = value.astype(BF)
    rest = value - high.astype(F32)
    middle = rest.astype(BF)
    return high, middle, (rest - middle.astype(F32)).astype(BF)


def stacked(value):
    high, low = split_2(value)
    return jnp.concatenate([high, low], axis=0)


def folded(value):
    half = value.shape[0] // 2
    return value[:half] + value[half:]


def dot(left, right):
    return jnp.dot(left, right, preferred_element_type=F32)


def one_hot(mask):
    return jnp.where(mask, 1.0, 0.0).astype(BF)


def padded_index(nodes, width, padded):
    block = jnp.floor((nodes + 0.5) * (1.0 / width))
    return nodes + block * (padded - width)


class Sizes:
    def __init__(self, inverse_blocks, voltage, wave_init, line_node, conv_node):
        self.blocks, self.picks, self.width, _ = inverse_blocks.shape
        self.scen, self.nodes = voltage.shape
        self.delays = wave_init.shape[0]
        self.ends = line_node.shape[0]
        self.lines = self.ends // 2
        self.convs = conv_node.shape[0]
        self.regions = lax.axis_size("region")
        self.capacity = max(2, 12 * self.convs // (5 * self.regions))
        self.rows = round_up(self.capacity + 4, 8)
        self.slots = self.regions * self.rows
        self.slot_lanes = round_up(self.slots, 2 * LANES)
        self.padded = round_up(self.width, LANES)
        self.lanes = self.blocks * self.padded
        self.group = math.lcm(self.width, LANES) // self.width

        self.state = (self.blocks, self.scen, self.padded)
        starts = [k * self.width for k in range(self.picks)]
        self.starts = starts
        self.shifts = sorted({start % LANES for start in starts})
        self.depth = round_up(self.picks * self.width, LANES)
        self.turned = (len(self.shifts), self.blocks, 2 * self.scen, self.padded)
        self.chunk = min(2 * LANES, self.slot_lanes)
        self.chunks = self.slot_lanes // self.chunk
        self.wide = (2 * self.scen, self.lanes)
        self.weights = (self.blocks, self.picks * self.width, 2 * self.padded)
        self.site_rows = (self.lanes, self.ends)
        self.response = (self.blocks, self.ends, 2 * self.padded)
        self.coupling = (self.ends, 2 * self.ends)
        self.node_rows = (self.blocks, 8, self.padded)
        self.fault_cols = (2, self.scen, self.padded)
        self.drive = (self.scen, self.ends)
        self.exchange = (self.scen, self.lines)


class Copies:
    def __init__(self, sems):
        self.sems = sems
        self.count = 0

    def start(self, source, target):
        copy = pltpu.make_async_copy(source, target, self.sems.at[self.count])
        self.count += 1
        copy.start()
        return copy


def pad_blocks(size, source, store):
    group_width = size.group * size.width
    for first in range(0, size.blocks, size.group):
        chunk = source[:, first * size.width : first * size.width + group_width]
        for j in range(size.group):
            part = chunk[:, j * size.width : (j + 1) * size.width]
            zeros = jnp.zeros((part.shape[0], size.padded - size.width), part.dtype)
            store(first + j, jnp.concatenate([part, zeros], axis=1))


def unpad_blocks(size, load, target):
    group_width = size.group * size.width
    for first in range(0, size.blocks, size.group):
        parts = [load(first + j)[:, : size.width] for j in range(size.group)]
        target[:, first * size.width : first * size.width + group_width] = jnp.concatenate(
            parts, axis=1
        )


def block_lanes(size, b):
    return slice(b * size.padded, (b + 1) * size.padded)


def pack_kernel(
    size, region_hbm, power_hbm, node_hbm, gains_hbm, init_hbm, out_hbm, dst_hbm,
    region, power, node, gains, init, out, dst_out, sems,
):
    convs, slots = size.convs, size.slots
    copies = Copies(sems)
    first = copies.start(region_hbm, region)
    second = copies.start(init_hbm, init)
    others = [
        copies.start(power_hbm, power),
        copies.start(node_hbm, node),
        copies.start(gains_hbm, gains),
    ]
    first.wait()
    target = region[...]
    member = iota((round_up(size.regions, 16), convs), 0) == target
    before = one_hot(iota((convs, convs), 0) < iota((convs, convs), 1))
    earlier = dot(one_hot(member), before)
    rank = jnp.sum(jnp.where(member, earlier, 0.0), axis=0, keepdims=True)
    dst = target * size.rows + rank.astype(I32)
    dst_out[...] = dst
    select = one_hot(iota((slots, convs), 0) == dst)
    sent = [copies.start(dst_out, dst_hbm)]
    for copy in others:
        copy.wait()
    rows = [
        power[...].reshape(1, convs),
        gains[...],
        node[...].astype(F32).reshape(1, convs) + 1.0,
        jnp.zeros((LANES - 4, convs), F32),
    ]
    settings = jnp.concatenate(rows, axis=0)
    second.wait()
    state = jnp.concatenate([init[0], init[1]], axis=0)
    payload = jnp.concatenate([state.T, settings.T], axis=1)
    width = state.shape[0]
    rows = sum(dot(select, part) for part in split_3(payload))
    for r in range(size.regions):
        chunk = rows[r * size.rows : (r + 1) * size.rows]
        out[r] = chunk[:, :width]
        filler = jnp.zeros((LANES - size.rows, LANES), F32)
        turned = jnp.concatenate([chunk[:, width:], filler], axis=0).T
        out[r, size.capacity : size.capacity + 4, :] = turned[:4]
    sent.append(copies.start(out, out_hbm))
    for copy in sent:
        copy.wait()


def fault_terms(size, node, kind):
    first = lax.axis_index("region") * size.nodes
    local = (node[...] - first).astype(F32)
    inside = (local >= 0.0) & (local < size.nodes)
    site = jnp.where(inside, padded_index(local, size.width, size.padded), -1.0)
    level = 0.25 * jnp.left_shift(1, kind[...]).astype(F32)
    square = (size.scen, size.scen)
    diagonal = iota(square, 0) == iota(square, 1)

    def column(row):
        spread = jnp.where(diagonal, jnp.broadcast_to(row, square), 0.0)
        return jnp.broadcast_to(jnp.sum(spread, axis=1, keepdims=True), (size.scen, size.padded))

    return column(site), column(level)


def site_products(size, row, chunk, gather, scatter):
    part = row[:, chunk : chunk + LANES]
    block = jnp.floor((part + 0.5) * (1.0 / LANES))
    lane = part - block * LANES
    square = (LANES, LANES)
    down_block = jnp.broadcast_to(block, square).astype(BF)
    across_block = turned_row(block).astype(BF)
    down_lane = one_hot(lane == iota(square, 0).astype(F32))
    across_lane = one_hot(turned_row(lane) == iota(square, 1).astype(F32))
    zeros = jnp.zeros(square, BF)
    for n in range(size.lanes // LANES):
        here = jnp.asarray(n, BF)
        gather(n, jnp.where(down_block == here, down_lane, zeros))
        scatter(n, jnp.where(across_block == here, across_lane, zeros))


def turned_row(row):
    return jnp.broadcast_to(row, (LANES, row.shape[1])).T


def put_turned(size, x, b, value):
    pair = stacked(value)
    for i, shift in enumerate(size.shifts):
        x[i, b] = pltpu.roll(pair, shift, 1) if shift else pair


def picked_product(size, cols, b, x, wp):
    lane = iota((2 * size.scen, LANES), 1)
    tiles = []
    for first in range(0, size.depth, LANES):
        tile = None
        for k, start in enumerate(size.starts):
            if start + size.width <= first or start >= first + LANES:
                continue
            piece = x[size.shifts.index(start % LANES), cols[k, b]]
            tile = piece if tile is None else jnp.where(lane < start - first, tile, piece)
        tiles.append(tile)
    spare = size.depth - size.picks * size.width
    weights = wp[b]
    if spare:
        weights = jnp.concatenate([weights, jnp.zeros((spare, weights.shape[1]), BF)], axis=0)
    return dot(jnp.concatenate(tiles, axis=1), weights)


def three_terms(product, rows, width):
    top, low = product[:rows], product[rows:]
    return top[:, :width] + top[:, width:] + low[:, :width]


def apply_inverse(size, cols, x, wp, volt, vb):
    def block_row(b, carry):
        value = three_terms(picked_product(size, cols, b, x, wp), size.scen, size.padded)
        volt[b] = value
        vb[:, pl.ds(pl.multiple_of(b * size.padded, LANES), size.padded)] = stacked(value)
        return carry

    lax.fori_loop(0, size.blocks, block_row, 0, unroll=16)


def prep_kernel(
    size,
    cols_hbm, inverse, source, decay, gain, voltage, branch_init, line_node, fault_node, fault_kind,
    wp_out, eg_out, mt_out, kk_out, vb_out, branch_out, rest_out, rows_out, fault_out,
    cols, raw, vectors, volt_in, branch_in, nodes, faults,
    wp, eg, es, mt, both, kk, vb, volt, branch, rest, node_rows, fault_cols,
    sems,
):
    copies = Copies(sems)
    cols_copy = copies.start(cols_hbm, cols)
    small = [
        copies.start(line_node, nodes),
        copies.start(fault_node, faults.at[0:1]),
        copies.start(fault_kind, faults.at[1:2]),
    ]
    small += [copies.start(v, vectors.at[i]) for i, v in enumerate((source, decay, gain))]
    large = [copies.start(voltage, volt_in), copies.start(branch_init, branch_in)]
    stages = 4
    stage = size.blocks // stages
    weight_copies = []
    for i in range(stages):
        part = pl.ds(i * stage, stage)
        weight_copies.append(copies.start(inverse.at[part], raw.at[part]))
    sent = []
    for copy in small:
        copy.wait()

    row = padded_index(nodes[...].astype(F32), size.width, size.padded)
    for c in range(0, size.ends, LANES):
        def put_gather(n, value, c=c):
            eg[n * LANES : (n + 1) * LANES, c : c + LANES] = value

        def put_scatter(n, value, c=c):
            b, lane = n * LANES // size.padded, n * LANES % size.padded
            es[b, c : c + LANES, lane : lane + LANES] = value

        site_products(size, row, c, put_gather, put_scatter)
    sent.append(copies.start(eg, eg_out))

    for i in range(3):
        def put_row(b, value, i=i):
            node_rows[b, i : i + 1, :] = value

        pad_blocks(size, vectors.at[i], put_row)
    sent.append(copies.start(node_rows, rows_out))
    site, level = fault_terms(size, faults.at[0:1], faults.at[1:2])
    fault_cols[0] = site
    fault_cols[1] = level
    sent.append(copies.start(fault_cols, fault_out))
    for copy in large:
        copy.wait()

    def put_voltage(b, value):
        volt[b] = value
        vb[:, block_lanes(size, b)] = stacked(value)

    def put_branch(b, value):
        history = node_rows[b, 1:2, :] * value + node_rows[b, 2:3, :] * volt[b]
        branch[b] = history
        rest[b] = rest_of(size, node_rows, b, history, volt[b], site, level)

    pad_blocks(size, volt_in, put_voltage)
    pad_blocks(size, branch_in, put_branch)
    sent.append(copies.start(vb, vb_out))
    sent.append(copies.start(branch, branch_out))
    sent.append(copies.start(rest, rest_out))

    cols_copy.wait()
    zeros = jnp.zeros((size.width, size.padded - size.width), BF)
    zero_rows = jnp.zeros((size.padded - size.width, 2 * size.padded), BF)
    for i, copy in enumerate(weight_copies):
        copy.wait()

        def turn(b, carry):
            parts = []
            for k in range(size.picks):
                high, low = split_2(raw[b, k].T)
                part = jnp.concatenate([high, zeros, low, zeros], axis=1)
                wp[b, k * size.width : (k + 1) * size.width, :] = part
                parts += [part, zero_rows]
            left = jnp.concatenate([es[cols[k, b]] for k in range(size.picks)], axis=1)
            product = dot(left, jnp.concatenate(parts, axis=0))
            high, low = split_2(product[:, : size.padded] + product[:, size.padded :])
            mt[b] = jnp.concatenate([high, low], axis=1)
            both[:, pl.ds(pl.multiple_of(b * size.padded, LANES), size.padded)] = jnp.concatenate(
                [high, low], axis=0
            )
            return carry

        lax.fori_loop(i * stage, (i + 1) * stage, turn, 0, unroll=4)
        part = pl.ds(i * stage, stage)
        sent.append(copies.start(wp.at[part], wp_out.at[part]))
        sent.append(copies.start(mt.at[part], mt_out.at[part]))

    high, low = split_2(folded(dot(both[...], eg[...])))
    kk[...] = jnp.concatenate([high, low], axis=1)
    sent.append(copies.start(kk, kk_out))
    for copy in sent:
        copy.wait()


def rest_of(size, node_rows, b, history, v, site, level):
    lane = iota((size.scen, size.padded), 1).astype(F32)
    first = jnp.asarray(b * size.padded, I32).astype(F32)
    hit = jnp.where(lane + first == site, level, 0.0)
    return node_rows[b, 0:1, :] - history - hit * v


def for_chunks(size, count, work):
    for c in range(size.chunks):
        if c < 2:
            work(c * size.chunk)
        else:
            pl.when(count > c)(functools.partial(work, c * size.chunk))


def inject(size, count, pair, cs, put):
    step = 2 if size.blocks % 2 == 0 else 1
    width = step * size.padded
    least = min(2, size.chunks)

    def inject_from(used):
        left = pair[:, : used * size.chunk]

        def some_blocks(i, carry):
            lanes = pl.ds(pl.multiple_of(i * width, LANES), width)
            both = folded(dot(left, cs[: used * size.chunk, lanes]))
            for j in range(step):
                put(i * step + j, both[:, block_lanes(size, j)])
            return carry

        lax.fori_loop(0, size.blocks // step, some_blocks, 0, unroll=True if used == least else 4)

    for used in range(least, size.chunks + 1):
        if used == least:
            chosen = count <= used
        else:
            chosen = count == used
        pl.when(chosen)(functools.partial(inject_from, used))


def converter_update(size, count, vb, cg, prm, filt, amps, pair):
    def update(first):
        lanes = slice(first, first + size.chunk)
        measured = folded(dot(vb[...], cg[:, lanes]))
        filtered = filt[:, lanes]
        filtered = filtered + prm[2:3, lanes] * (measured - filtered)
        current = amps[:, lanes]
        target = prm[0:1, lanes] * filtered / (1.0 + filtered * filtered)
        current = current + prm[1:2, lanes] * (target - current)
        filt[:, lanes] = filtered
        amps[:, lanes] = current
        pair[:, lanes] = stacked(current)

    for_chunks(size, count, update)


def launch_part(size, history, ends, at_ends, kk, drive_out, far, near):
    drive = jnp.zeros(size.drive, F32)
    for d in range(size.delays):
        drive = jnp.where(ends[0:1, :] == float(d + 1), history(d), drive)
    drive_out[...] = drive
    answer = three_terms(dot(stacked(drive), kk[...]), size.scen, size.ends)
    launch = 2.0 * ends[1:2, :] * (at_ends + answer) - drive
    even = lax.rem(lax.axis_index("region"), 2) == 0
    up, down = launch[:, size.lines :], launch[:, : size.lines]
    far[...] = jnp.where(even, down, up)
    near[...] = jnp.where(even, up, down)


def arrived(size, far, near):
    even = lax.rem(lax.axis_index("region"), 2) == 0
    ahead = jnp.where(even, far[...], near[...])
    after = jnp.where(even, near[...], far[...])
    return jnp.concatenate([ahead, after], axis=1)


def start_kernel(
    size,
    cols_hbm, received, waves_hbm, delay_hbm, admittance_hbm,
    wp_hbm, eg_hbm, mt_hbm, kk_hbm, vb_hbm, branch_hbm, rest_hbm, rows_hbm, fault_hbm,
    wp, eg, mt, kk, waves, ends, node_rows, fault_cols, branch, cg, cs, prm, filt, amps, volt,
    peak, drive, far, near, place_hbm,
    cols, place, delays, admittances, rest, x, vb, pair, moved, moved_settings, sems,
):
    copies = Copies(sems)
    vb_copy = copies.start(vb_hbm, vb)
    rest_copy = copies.start(rest_hbm, rest)
    cols_copy = copies.start(cols_hbm, cols)
    wp_copy = copies.start(wp_hbm, wp)
    later = [
        copies.start(eg_hbm, eg),
        copies.start(delay_hbm, delays),
        copies.start(admittance_hbm, admittances),
        copies.start(waves_hbm, waves),
        copies.start(kk_hbm, kk),
        copies.start(mt_hbm, mt),
        copies.start(branch_hbm, branch),
        copies.start(rows_hbm, node_rows),
        copies.start(fault_hbm, fault_cols),
    ]
    rows, capacity, slots, regions = size.rows, size.capacity, size.slots, size.regions
    total = 0
    for r in range(regions):
        settings = received[r * rows + capacity : r * rows + capacity + 4, :]
        filler = jnp.zeros((LANES - 4, LANES), F32)
        turned = jnp.concatenate([settings[:, :LANES], filler], axis=0).T
        place[r] = total
        moved[pl.ds(total, rows), :] = received[r * rows : (r + 1) * rows, :]
        moved_settings[pl.ds(total, rows), :] = turned[:rows]
        total = total + jnp.sum(jnp.where(settings[3:4, :] > 0.0, 1.0, 0.0)).astype(I32)
    count = lax.div(total + (size.chunk - 1), size.chunk)
    place[regions] = count
    place_copy = copies.start(place, place_hbm)
    for c in range(0, size.slot_lanes, LANES):
        valid = iota((LANES, LANES), 0) + c < total
        turned = jnp.where(valid, moved[c : c + LANES, :], 0.0).T
        filt[:, c : c + LANES] = turned[: size.scen]
        amps[:, c : c + LANES] = turned[size.scen :]
        turned = jnp.where(valid, moved_settings[c : c + LANES, :], 0.0).T
        prm[:, c : c + LANES] = turned[:8]
    row = padded_index(prm[3:4, :] - 1.0, size.width, size.padded)

    def put_products(first):
        for c in range(first, first + size.chunk, LANES):
            def put_gather(n, value, c=c):
                cg[n * LANES : (n + 1) * LANES, c : c + LANES] = value

            def put_scatter(n, value, c=c):
                cs[c : c + LANES, n * LANES : (n + 1) * LANES] = value

            site_products(size, row, c, put_gather, put_scatter)

    for_chunks(size, count, put_products)
    peak[...] = jnp.zeros(peak.shape, F32)

    vb_copy.wait()
    converter_update(size, count, vb, cg, prm, filt, amps, pair)
    rest_copy.wait()

    def put_start(b, injected):
        put_turned(size, x, b, rest[b] + injected)

    inject(size, count, pair, cs, put_start)
    cols_copy.wait()
    wp_copy.wait()
    apply_inverse(size, cols, x, wp, volt, vb)
    for copy in later:
        copy.wait()
    ends[0:1, :] = delays[...].astype(F32)
    ends[1:2, :] = admittances[...]
    at_ends = folded(dot(vb[...], eg[...]))
    launch_part(size, lambda d: waves[d], ends, at_ends, kk, drive, far, near)
    place_copy.wait()


def middle_kernel(
    size, last,
    cols_hbm, place_hbm, drive, wp, eg, mt, node_rows, fault_cols, cg, cs, prm,
    branch_in, filt_in, amps_in, volt_in, peak_in,
    branch, filt, amps, volt, peak, at_ends, *refs,
):
    if last:
        back_hbm, branch_hbm, volt_hbm, peak_hbm, branch_out, moved, back = *refs[:4], *refs[-3:]
        refs = refs[4:-3]
    cols, place, x, vb, pair, sems = refs
    copies = Copies(sems)
    place_copy = copies.start(place_hbm, place)
    cols_copy = copies.start(cols_hbm, cols)
    drives = stacked(drive[...])
    for b in range(size.blocks):
        added = three_terms(dot(drives, mt[b]), size.scen, size.padded)
        v = volt[b] + added
        volt[b] = v
        vb[:, block_lanes(size, b)] = stacked(v)
        magnitude = jnp.abs(v)
        top = magnitude[:8]
        for s in range(8, size.scen, 8):
            top = jnp.maximum(top, magnitude[s : s + 8])
        peak[b] = jnp.maximum(peak[b], top)
    place_copy.wait()
    count = place[size.regions]
    converter_update(size, count, vb, cg, prm, filt, amps, pair)

    def put_next(b, injected):
        history = node_rows[b, 1:2, :] * branch[b] + node_rows[b, 2:3, :] * volt[b]
        branch[b] = history
        site, level = fault_cols[0], fault_cols[1]
        rest = rest_of(size, node_rows, b, history, volt[b], site, level)
        put_turned(size, x, b, rest + injected)

    inject(size, count, pair, cs, put_next)
    cols_copy.wait()
    if last:
        for c in range(0, size.slot_lanes, LANES):
            part = jnp.concatenate([filt[:, c : c + LANES], amps[:, c : c + LANES]], axis=0)
            moved[c : c + LANES, :] = part.T
        moved[size.slot_lanes :, :] = jnp.zeros((size.rows, 2 * size.scen), F32)
        for r in range(size.regions):
            back[r * size.rows : (r + 1) * size.rows, :] = moved[pl.ds(place[r], size.rows), :]
        unpad_blocks(size, lambda b: branch[b], branch_out)
        sent = [
            copies.start(back, back_hbm),
            copies.start(branch_out, branch_hbm),
            copies.start(peak, peak_hbm),
        ]
    apply_inverse(size, cols, x, wp, volt, vb)
    if last:
        sent.append(copies.start(volt, volt_hbm))
    at_ends[...] = folded(dot(vb[...], eg[...]))
    if last:
        for copy in sent:
            copy.wait()


def launch_kernel(size, done, last, at_ends, kk, ends, waves, *refs):
    arrivals, refs = refs[: 2 * done], refs[2 * done :]

    def history(d):
        if d >= done:
            return waves[d - done]
        return arrived(size, arrivals[2 * d], arrivals[2 * d + 1])

    if last:
        refs = refs[1:]
    drive, far, near = refs[:3]
    if last:
        drive_hbm = drive
        _, waves_out, recent, drive, sems = refs[3:]
        copies = Copies(sems)
        for d in range(done):
            recent[d] = history(d)
        sent = [copies.start(recent, waves_out.at[pl.ds(1, done)])]
        kept = size.delays - 1 - done
        sent.append(copies.start(waves.at[pl.ds(0, kept)], waves_out.at[pl.ds(1 + done, kept)]))
    launch_part(size, history, ends, at_ends[...], kk, drive, far, near)
    if last:
        sent.append(copies.start(drive, drive_hbm))
        for copy in sent:
            copy.wait()


def final_kernel(
    size, drive_hbm, volt_hbm, mt_hbm, peak_hbm, voltage_hbm, top_hbm,
    drive, volt, mt, peak, voltage_out, peak_row, peak_out, sems,
):
    copies = Copies(sems)
    drive_copy = copies.start(drive_hbm, drive)
    half = size.blocks // 2
    parts = []
    for i in range(2):
        part = pl.ds(i * half, half)
        parts.append(
            [copies.start(volt_hbm.at[part], volt.at[part]), copies.start(mt_hbm.at[part], mt.at[part])]
        )
    peak_copy = copies.start(peak_hbm, peak)
    drive_copy.wait()
    pair = stacked(drive[...])
    for b in range(size.blocks):
        if b % half == 0:
            for copy in parts[b // half]:
                copy.wait()
        volt[b] = volt[b] + three_terms(dot(pair, mt[b]), size.scen, size.padded)
    peak_copy.wait()

    def largest(b):
        top = jnp.max(jnp.abs(volt[b]), axis=0, keepdims=True)
        return jnp.maximum(top, jnp.max(peak[b], axis=0, keepdims=True))

    unpad_blocks(size, largest, peak_row)
    for i in range(peak_out.shape[0]):
        peak_out[i : i + 1, :] = peak_row[:, i * LANES : (i + 1) * LANES]
    sent = [copies.start(peak_out, top_hbm)]
    unpad_blocks(size, lambda b: volt[b], voltage_out)
    sent.append(copies.start(voltage_out, voltage_hbm))
    for copy in sent:
        copy.wait()


def end_kernel(
    size, dst_hbm, received, far, near, waves_in, state_hbm, waves_out,
    dst, newest, state_out, sems,
):
    copies = Copies(sems)
    dst_copy = copies.start(dst_hbm, dst)
    newest[0] = arrived(size, far, near)
    sent = [copies.start(newest, waves_out.at[pl.ds(0, 1)])]
    parts = jnp.concatenate(split_3(received[...].T), axis=0)
    dst_copy.wait()
    select = one_hot(iota((size.slots, size.convs), 0) == dst[...])
    state = dot(parts, select)
    width = 2 * size.scen
    state = state[:width] + state[width : 2 * width] + state[2 * width :]
    state_out[0] = state[: size.scen]
    state_out[1] = state[size.scen :]
    sent.append(copies.start(state_out, state_hbm))
    for copy in sent:
        copy.wait()


def shape(dims, dtype=F32):
    return jax.ShapeDtypeStruct(dims, dtype)


def in_vmem(*values):
    return [pltpu.with_memory_space_constraint(v, pltpu.VMEM) for v in values]


def in_hbm(*values):
    return [pltpu.with_memory_space_constraint(v, pltpu.HBM) for v in values]


def call(kernel, name, outs, out_specs, args, specs, scratch, limit, aliases=None):
    return pl.pallas_call(
        kernel,
        name=name,
        out_shape=outs,
        in_specs=specs,
        out_specs=out_specs,
        scratch_shapes=list(scratch),
        input_output_aliases=aliases or {},
        compiler_params=pltpu.CompilerParams(vmem_limit_bytes=limit << 20),
    )(*args)


def shards(
    inverse_blocks, block_cols, source_current, node_decay, node_gain, voltage_init, branch_init,
    wave_init, line_node, line_delay, line_admittance, conv_region, conv_node, conv_power,
    conv_gains, conv_init, fault_node, fault_kind,
):
    size = Sizes(inverse_blocks, voltage_init, wave_init, line_node, conv_node)
    regions, rows, scen = size.regions, size.rows, size.scen
    near_pairs = [(i, i ^ 1) for i in range(regions)]
    far_pairs = [(i, (i - 1 if i % 2 == 0 else i + 1) % regions) for i in range(regions)]
    dma = pltpu.SemaphoreType.DMA
    vmem, hbm = pltpu.VMEM, pltpu.HBM

    def row(vector):
        return vector.reshape(1, -1)

    chunk = (regions, rows, 2 * scen)
    packed, dst = call(
        functools.partial(pack_kernel, size),
        "pack",
        [hbm(chunk, F32), hbm((1, size.convs), I32)],
        [HBM] * 2,
        in_hbm(row(conv_region), conv_power, conv_node, conv_gains, conv_init),
        [HBM] * 5,
        [
            vmem((1, size.convs), I32),
            vmem(conv_power.shape, F32),
            vmem(conv_node.shape, I32),
            vmem(conv_gains.shape, F32),
            vmem(conv_init.shape, F32),
            vmem(chunk, F32),
            vmem((1, size.convs), I32),
            dma((8,)),
        ],
        16,
    )
    received = lax.all_to_all(packed, "region", split_axis=0, concat_axis=0, tiled=True)
    received = received.reshape(size.slots, 2 * scen)

    cols = block_cols.T
    cols_scratch = pltpu.SMEM(cols.shape, I32)
    x_scratch = vmem(size.turned, BF)
    wide_scratch = vmem(size.wide, BF)
    place_scratch = pltpu.SMEM((LANES,), I32)
    pair_scratch = vmem((2 * scen, size.slot_lanes), BF)
    moved_scratch = vmem((size.slot_lanes + rows, 2 * scen), F32)
    kept = [
        (size.weights, BF),
        (size.site_rows, BF),
        (size.response, BF),
        (size.coupling, BF),
        (size.wide, BF),
        (size.state, F32),
        (size.state, F32),
        (size.node_rows, F32),
        (size.fault_cols, F32),
    ]
    vectors = (3, 1, size.nodes)
    args = [
        cols, inverse_blocks, row(source_current), row(node_decay), row(node_gain), voltage_init,
        branch_init, row(line_node), row(fault_node), row(fault_kind),
    ]
    wp_hbm, eg_hbm, mt_hbm, kk_hbm, vb_hbm, branch_hbm, rest_hbm, rows_hbm, fault_hbm = call(
        functools.partial(prep_kernel, size),
        "prep",
        [hbm(*item) for item in kept],
        [HBM] * len(kept),
        in_hbm(*args),
        [HBM] * len(args),
        [
            cols_scratch,
            vmem(inverse_blocks.shape, F32),
            vmem(vectors, F32),
            vmem(voltage_init.shape, F32),
            vmem(voltage_init.shape, F32),
            vmem((1, size.ends), I32),
            vmem((2, scen), I32),
            vmem(size.weights, BF),
            vmem(size.site_rows, BF),
            vmem((size.blocks, size.ends, size.padded), BF),
            vmem(size.response, BF),
            vmem((2 * size.ends, size.lanes), BF),
            vmem(size.coupling, BF),
            wide_scratch,
            vmem(size.state, F32),
            vmem(size.state, F32),
            vmem(size.state, F32),
            vmem(size.node_rows, F32),
            vmem(size.fault_cols, F32),
            dma((40,)),
        ],
        48,
    )

    slot_state = vmem((scen, size.slot_lanes), F32)
    outs = [
        vmem(size.weights, BF),
        vmem(size.site_rows, BF),
        vmem(size.response, BF),
        vmem(size.coupling, BF),
        vmem(wave_init.shape, F32),
        vmem((8, size.ends), F32),
        vmem(size.node_rows, F32),
        vmem(size.fault_cols, F32),
        vmem(size.state, F32),
        vmem((size.lanes, size.slot_lanes), BF),
        vmem((size.slot_lanes, size.lanes), BF),
        vmem((8, size.slot_lanes), F32),
        slot_state,
        slot_state,
        vmem(size.state, F32),
        vmem(size.node_rows, F32),
        vmem(size.drive, F32),
        shape(size.exchange),
        shape(size.exchange),
        hbm((LANES,), I32),
    ]
    args = [
        cols, received, wave_init, row(line_delay), row(line_admittance), wp_hbm, eg_hbm,
        mt_hbm, kk_hbm, vb_hbm, branch_hbm, rest_hbm, rows_hbm, fault_hbm,
    ]
    (
        wp, eg, mt, kk, waves, ends, node_rows, fault_cols, branch, cg, cs, prm, filt, amps, volt,
        peak, drive, far, near, place,
    ) = call(
        functools.partial(start_kernel, size),
        "start",
        outs,
        [VMEM] * (len(outs) - 1) + [HBM],
        in_hbm(cols) + in_vmem(received) + in_hbm(*args[2:]),
        [HBM, VMEM] + [HBM] * (len(args) - 2),
        [
            cols_scratch,
            place_scratch,
            vmem((1, size.ends), I32),
            vmem((1, size.ends), F32),
            vmem(size.state, F32),
            x_scratch,
            wide_scratch,
            pair_scratch,
            moved_scratch,
            moved_scratch,
            dma((16,)),
        ],
        10,
    )

    arrivals = []
    for step in range(1, STEPS):
        last = step == STEPS - 1
        from_far = lax.ppermute(far, "region", far_pairs)
        from_near = lax.ppermute(near, "region", near_pairs)
        outs = [
            vmem(size.state, F32),
            slot_state,
            slot_state,
            vmem(size.state, F32),
            vmem(size.node_rows, F32),
            vmem(size.drive, F32),
        ]
        specs = [VMEM] * len(outs)
        scratch = [cols_scratch, place_scratch, x_scratch, wide_scratch, pair_scratch, dma((6,))]
        if last:
            outs += [
                hbm((size.slots, 2 * scen), F32),
                hbm((scen, size.nodes), F32),
                hbm(size.state, F32),
                hbm(size.node_rows, F32),
            ]
            specs += [HBM] * 4
            scratch += [
                vmem((scen, size.nodes), F32),
                moved_scratch,
                vmem((size.slots, 2 * scen), F32),
            ]
        result = call(
            functools.partial(middle_kernel, size, last),
            "middle",
            outs,
            specs,
            in_hbm(cols, place)
            + in_vmem(
                drive, wp, eg, mt, node_rows, fault_cols, cg, cs, prm, branch, filt, amps, volt, peak
            ),
            [HBM] * 2 + [VMEM] * 14,
            scratch,
            12,
            {11: 0, 12: 1, 13: 2, 14: 3, 15: 4},
        )
        branch, filt, amps, volt, peak, at_ends = result[:6]
        arrivals = [from_far, from_near] + arrivals
        args = in_vmem(at_ends, kk, ends, waves) + arrivals
        outs = [vmem(size.drive, F32), shape(size.exchange), shape(size.exchange)]
        in_specs, specs, scratch, aliases = [VMEM] * len(args), [VMEM] * 3, [], {}
        if last:
            back, branch_out, volt, peak = result[6:]
            aliases = {len(args): 3}
            args += in_hbm(back)
            in_specs.append(HBM)
            outs[0] = hbm(size.drive, F32)
            outs += [hbm((size.slots, 2 * scen), F32), hbm(wave_init.shape, F32)]
            specs[0] = HBM
            specs += [HBM, HBM]
            scratch = [vmem((step, *size.drive), F32), vmem(size.drive, F32), dma((4,))]
        drive, far, near, *rest = call(
            functools.partial(launch_kernel, size, step, last),
            "launch",
            outs,
            specs,
            args,
            in_specs,
            scratch,
            4,
            aliases,
        )
    chunks, waves_out = rest
    from_far = lax.ppermute(far, "region", far_pairs)
    from_near = lax.ppermute(near, "region", near_pairs)
    chunks = chunks.reshape(regions, rows, 2 * scen)
    returned = lax.all_to_all(chunks, "region", split_axis=0, concat_axis=0, tiled=True)
    voltage_out, peak_out = call(
        functools.partial(final_kernel, size),
        "final",
        [hbm((scen, size.nodes), F32), hbm((size.nodes // LANES, LANES), F32)],
        [HBM] * 2,
        in_hbm(drive, volt, mt_hbm, peak),
        [HBM] * 4,
        [
            vmem(size.drive, F32),
            vmem(size.state, F32),
            vmem(size.response, BF),
            vmem(size.node_rows, F32),
            vmem((scen, size.nodes), F32),
            vmem((1, size.nodes), F32),
            vmem((size.nodes // LANES, LANES), F32),
            dma((8,)),
        ],
        12,
    )
    others = lax.axis_size("scen")
    peaks = []
    for d in range(1, others):
        if others & (others - 1):
            shift = [(i, (i + d) % others) for i in range(others)]
        else:
            shift = [(i, i ^ d) for i in range(others)]
        peaks.append(lax.ppermute(peak_out, "scen", shift))
    returned = returned.reshape(size.slots, 2 * scen)
    conv_state, wave_history = call(
        functools.partial(end_kernel, size),
        "end",
        [hbm(conv_init.shape, F32), hbm(wave_init.shape, F32)],
        [HBM] * 2,
        in_hbm(dst) + in_vmem(returned, from_far, from_near) + in_hbm(waves_out),
        [HBM, VMEM, VMEM, VMEM, HBM],
        [
            vmem(dst.shape, I32),
            vmem((1, *size.drive), F32),
            vmem(conv_init.shape, F32),
            dma((3,)),
        ],
        16,
        {4: 1},
    )
    envelope, conv_state = lax.optimization_barrier((peak_out, conv_state))
    for peak in peaks:
        envelope = jnp.maximum(envelope, peak)
    return voltage_out, branch_out, wave_history, conv_state, envelope.reshape(-1)


def solution(mesh):
    placed = (
        P("region", None, None, None),
        P("region", None),
        P("region"),
        P("region"),
        P("region"),
        P("scen", "region"),
        P("scen", "region"),
        P(None, "scen", "region"),
        P("region"),
        P("region"),
        P("region"),
        P("region", None),
        P("region"),
        P("region"),
        P(None, "region"),
        P(None, "scen", "region"),
        P("scen"),
        P("scen"),
    )
    return jax.shard_map(
        shards,
        mesh=mesh,
        in_specs=placed,
        out_specs=(
            P("scen", "region"),
            P("scen", "region"),
            P(None, "scen", "region"),
            P(None, "scen", "region"),
            P("region"),
        ),
        check_vma=False,
    )
```

profile of v0, /device:TPU:0, one launch (start us, length us, event | category | flops | bytes accessed | tf_op | source)
XLA Modules:
  0.0 80.0 jit_solution(16170427696946048730)
XLA Ops:
  0.6 3.0 %pack.1 = (f32[8,120,128]{2,1,0:T(8,128)}, s32[1,384]{1,0:T(1,128)}) custom-call(s32[1,384]{1,0:T(1,128)} %bitcast.26, f32[384]{0:T(512)} %power_hbm.1, s32[384]{0:T(512)} %node_hbm.1, f32[2,384]{1,0:T(2,128)} %gains_hbm.1, f32[2,64,384]{2,1,0:T(8,128)} %init_hbm.1), custom_call_target="tpu_custom_call" | custom-call | tf_op jit(solution)/shard_map/pack/pallas_call | solution.py:671
  3.7 7.3 %all-to-all-start = ((f32[8,120,128]{2,1,0:T(8,128)}), f32[8,120,128]{2,1,0:T(8,128)S(1)}, u32[]{:S(2)}, u32[]{:S(2)}) async-start(f32[8,120,128]{2,1,0:T(8,128)} %get-tuple-element.70), calls=%async_computation | async-start | bytes 983040 | tf_op jit(solution)/shard_map/all_to_all | solution.py:718
  11.0 10.8 %prep.1 = (bf16[32,480,256]{2,1,0:T(8,128)(2,1)}, bf16[4096,256]{1,0:T(8,128)(2,1)}, bf16[32,256,256]{2,1,0:T(8,128)(2,1)}, bf16[256,512]{1,0:T(8,128)(2,1)}, bf...) custom-call(s32[5,32]{1,0:T(8,128)} %bitcast.18, ...), custom_call_target="tpu_custom_call" | custom-call | tf_op jit(solution)/shard_map/prep/pallas_call | solution.py:671
  21.7 3.0 %all-to-all-done = f32[8,120,128]{2,1,0:T(8,128)S(1)} async-done(((f32[8,120,128]{2,1,0:T(8,128)}), f32[8,120,128]{2,1,0:T(8,128)S(1)}, u32[]{:S(2)}, u32[]{:S(2)}) %all-to-all-start) | async-done | bytes 491552 | tf_op jit(solution)/shard_map/all_to_all | solution.py:718
  24.7 7.0 %start.1 = (bf16[32,480,256]{2,1,0:T(8,128)(2,1)S(1)}, bf16[4096,256]{1,0:T(8,128)(2,1)S(1)}, bf16[32,256,256]{2,1,0:T(8,128)(2,1)S(1)}, bf16[256,512]{1,0:T(8,1...) custom-call(s32[5,32]{1,0:T(8,128)} %bitcast.19, ...), custom_call_target="tpu_custom_call" | custom-call | tf_op jit(solution)/shard_map/start/pallas_call | solution.py:671
  31.8 2.4 %collective-permute-start = (f32[64,128]{1,0:T(8,128)S(1)}, f32[64,128]{1,0:T(8,128)S(1)}, u32[]{:S(2)}, u32[]{:S(2)}) collective-permute-start(f32[64,128]{1,0:T(8,128)S(1)} %get-tuple-element.99), channel_id=1, source_target_pairs={{0,28},{4,8},{8,4},{12,16},{16,12},{20,24},{24,20},{28,0},{1,29},{... | collective-permute-start | bytes 98312 | tf_op jit(solution)/shard_map/ppermute | solution.py:832
  34.2 0.0 collective-permute-start.1
  34.2 5.4 %middle.3 = (f32[32,64,128]{2,1,0:T(8,128)S(1)}, f32[64,1024]{1,0:T(8,128)S(1)}, f32[64,1024]{1,0:T(8,128)S(1)}, f32[32,64,128]{2,1,0:T(8,128)S(1)}, f32[32,8,128]{2,1,0:T(8,128)S(1)}, /*index=5*/f32[64,256]{1,0:T(8,128)S(1)}) custom-call(s32[5,32]{1,0:T(8,128)} %bitcast.20, ...), custom_call_target="tpu_custom_call", output_to_operand_aliasing={{0}: (11, {}), {1}: (12, {}), {2}: (13, {}), {3}: (14, {}),... | custom-call | tf_op jit(solution)/shard_map/middle/pallas_call | solution.py:671
  39.6 0.2 launch.3
  39.8 2.8 %collective-permute-start.2 = (f32[64,128]{1,0:T(8,128)S(1)}, f32[64,128]{1,0:T(8,128)S(1)}, u32[]{:S(2)}, u32[]{:S(2)}) collective-permute-start(f32[64,128]{1,0:T(8,128)S(1)} %get-tuple-element.108), channel_id=1, source_target_pairs={{0,28},{4,8},{8,4},{12,16},{16,12},{20,24},{24,20},{28,0},{1,29},{... | collective-permute-start | bytes 98312 | tf_op jit(solution)/shard_map/ppermute | solution.py:832
  42.6 5.6 %middle.4 = (f32[32,64,128]{2,1,0:T(8,128)S(1)}, f32[64,1024]{1,0:T(8,128)S(1)}, f32[64,1024]{1,0:T(8,128)S(1)}, f32[32,64,128]{2,1,0:T(8,128)S(1)}, f32[32,8,128]{2,1,0:T(8,128)S(1)}, /*index=5*/f32[64,256]{1,0:T(8,128)S(1)}) custom-call(s32[5,32]{1,0:T(8,128)} %bitcast.21, ...), custom_call_target="tpu_custom_call", output_to_operand_aliasing={{0}: (11, {}), {1}: (12, {}), {2}: (13, {}), {3}: (14, {}),... | custom-call | tf_op jit(solution)/shard_map/middle/pallas_call | solution.py:671
  48.3 0.0 collective-permute-done.3.refs_1_.refs_3_
  48.3 0.2 launch.4
  48.5 3.5 %collective-permute-start.4 = (f32[64,128]{1,0:T(8,128)S(1)}, f32[64,128]{1,0:T(8,128)S(1)}, u32[]{:S(2)}, u32[]{:S(2)}) collective-permute-start(f32[64,128]{1,0:T(8,128)S(1)} %get-tuple-element.117), channel_id=1, source_target_pairs={{0,28},{4,8},{8,4},{12,16},{16,12},{20,24},{24,20},{28,0},{1,29},{... | collective-permute-start | bytes 98312 | tf_op jit(solution)/shard_map/ppermute | solution.py:832
  52.0 0.6 collective-permute-start.5
  52.5 6.4 %middle.5 = (f32[32,64,128]{2,1,0:T(8,128)S(1)}, f32[64,1024]{1,0:T(8,128)S(1)}, f32[64,1024]{1,0:T(8,128)S(1)}, f32[32,64,128]{2,1,0:T(8,128)S(1)}, f32[32,8,12...) custom-call(s32[5,32]{1,0:T(8,128)} %bitcast.22, ...), custom_call_target="tpu_custom_call", output_to_operand_aliasing={{0}: (11, {}), {1}: (12, {}), {2}: (13, {}), {3}: (14, {}),... | custom-call | tf_op jit(solution)/shard_map/middle/pallas_call | solution.py:671
  59.0 0.0 collective-permute-done.4.refs_0_
  59.0 0.8 %launch.5 = (f32[64,256]{1,0:T(8,128)}, f32[64,128]{1,0:T(8,128)S(1)}, f32[64,128]{1,0:T(8,128)S(1)}, f32[960,128]{1,0:T(8,128)}, f32[8,64,256]{2,1,0:T(8,128)}) custom-call(f32[64,256]{1,0:T(8,128)S(1)} %get-tuple-element.116.at_ends, bf16[256,512]{1,0:T(8,128)(2,1)S(1)} %get-tuple-element.96.kk, ...), custom_call_target="tpu_custom_call", output_to_operand_aliasing={{3}: (10, {})} | custom-call | tf_op jit(solution)/shard_map/launch/pallas_call | solution.py:671
  59.8 4.3 %all-to-all-start.1 = ((f32[8,120,128]{2,1,0:T(8,128)}), f32[8,120,128]{2,1,0:T(8,128)S(1)}, u32[]{:S(2)}, u32[]{:S(2)}) async-start(f32[8,120,128]{2,1,0:T(8,128)} %bitcast.17), calls=%async_computation.1 | async-start | bytes 983040 | tf_op jit(solution)/shard_map/all_to_all | solution.py:901
  64.1 4.7 %collective-permute-start.6 = (f32[64,128]{1,0:T(8,128)S(1)}, f32[64,128]{1,0:T(8,128)S(1)}, u32[]{:S(2)}, u32[]{:S(2)}) collective-permute-start(f32[64,128]{1,0:T(8,128)S(1)} %get-tuple-element.127), channel_id=1, source_target_pairs={{0,28},{4,8},{8,4},{12,16},{16,12},{20,24},{24,20},{28,0},{1,29},{... | collective-permute-start | bytes 98312 | tf_op jit(solution)/shard_map/ppermute | solution.py:898
  68.8 0.0 collective-permute-start.7
  68.8 4.3 %final.1 = (f32[64,3072]{1,0:T(8,128)}, f32[24,128]{1,0:T(8,128)}) custom-call(f32[64,256]{1,0:T(8,128)} %get-tuple-element.120.drive_hbm, f32[32,64,128]{2,1,0:T(8,128)} %get-tuple-element.121.volt_hbm, bf16[32,256,256]{2,1,0:T(8,128)(2,1)} %get-tuple-element.73.mt_hbm, f32[32,8,128]{2,1,0:T(8,128)} %get-tuple-element.122.peak_hbm), custom_call_target="tpu_custom_call" | custom-call | tf_op jit(solution)/shard_map/final/pallas_call | solution.py:671
  73.2 0.1 collective-permute-start.10
  73.3 1.6 %collective-permute-start.9 = (f32[24,128]{1,0:T(8,128)}, f32[24,128]{1,0:T(8,128)S(1)}, u32[]{:S(2)}, u32[]{:S(2)}) collective-permute-start(f32[24,128]{1,0:T(8,128)} %get-tuple-element.134), channel_id=1, source_target_pairs={{0,2},{1,3},{2,0},{3,1},{4,6},{5,7},{6,4},{7,5},{8,10},{9,11},{10,... | collective-permute-start | bytes 36872 | tf_op jit(solution)/shard_map/ppermute | solution.py:928
  74.8 0.3 collective-permute-start.8
  75.1 1.2 %collective-permute-done.6.far = f32[64,128]{1,0:T(8,128)S(1)} collective-permute-done((f32[64,128]{1,0:T(8,128)S(1)}, f32[64,128]{1,0:T(8,128)S(1)}, u32[]{:S(2)}, u32[]{:S(2)}) %collective-permute-start.6) | collective-permute-done | bytes 32800 | tf_op jit(solution)/shard_map/ppermute | solution.py:898
  76.3 0.0 collective-permute-done.7.near
  76.3 0.4 all-to-all-done.1
  76.7 2.0 %end.1 = (f32[2,64,384]{2,1,0:T(8,128)}, f32[8,64,256]{2,1,0:T(8,128)}) custom-call(s32[1,384]{1,0:T(1,128)} %get-tuple-element.125.dst_hbm, f32[960,128]{1,0:T(8,128)S(1)} %bitcast.15, f32[64,128]{1,0:T(8,128)S(1)} %collective-permute-done.6.far, f32[64,128]{1,0:T(8,128)S(1)} %collective-permute-done.7.near, ...), custom_call_target="tpu_custom_call", output_to_operand_aliasing={{1}: (4, {})} | custom-call | tf_op jit(solution)/shard_map/end/pallas_call | solution.py:671
  78.7 0.0 collective-permute-done.10
  78.7 0.0 collective-permute-done.8
  78.7 1.3 %maximum_bitcast_fusion = f32[3072]{0:T(1024)} fusion(f32[24,128]{1,0:T(8,128)S(1)} %collective-permute-done.10, f32[24,128]{1,0:T(8,128)S(1)} %collective-permute-done.9, f32[24,128]{1,0:T(8,128)} %get-tuple-element.134, f32[24,128]{1,0:T(8,128)S(1)} %collective-permute-done.8), kind=kLoop, calls=%fused_computation | loop fusion | flops 9216 | bytes 61440 | tf_op jit(solution)/shard_map/reshape | solution.py:949
  (6 shorter events, 0.0 us)
Async XLA Ops:
  3.7 21.1 %all-to-all-start = ((f32[8,120,128]{2,1,0:T(8,128)}), f32[8,120,128]{2,1,0:T(8,128)S(1)}, u32[]{:S(2)}, u32[]{:S(2)}) async-start(f32[8,120,128]{2,1,0:T(8,128)} %get-tuple-element.70), calls=%async_computation | async-start | bytes 983040 | tf_op jit(solution)/shard_map/all_to_all | solution.py:718
  31.8 7.8 %collective-permute-start = (f32[64,128]{1,0:T(8,128)S(1)}, f32[64,128]{1,0:T(8,128)S(1)}, u32[]{:S(2)}, u32[]{:S(2)}) collective-permute-start(f32[64,128]{1,0:T(8,128)S(1)} %get-tuple-element.99), channel_id=1, source_target_pairs={{0,28},{4,8},{8,4},{12,16},{16,12},{20,24},{24,20},{28,0},{1,29},{... | collective-permute-start | bytes 98312 | tf_op jit(solution)/shard_map/ppermute | solution.py:832
  34.2 5.4 %collective-permute-start.1 = (f32[64,128]{1,0:T(8,128)S(1)}, f32[64,128]{1,0:T(8,128)S(1)}, u32[]{:S(2)}, u32[]{:S(2)}) collective-permute-start(f32[64,128]{1,0:T(8,128)S(1)} %get-tuple-element.100), channel_id=1, source_target_pairs={{0,4},{4,0},{8,12},{12,8},{16,20},{20,16},{24,28},{28,24},{1,5},{5... | collective-permute-start | bytes 98312 | tf_op jit(solution)/shard_map/ppermute | solution.py:833
  39.8 8.4 %collective-permute-start.2 = (f32[64,128]{1,0:T(8,128)S(1)}, f32[64,128]{1,0:T(8,128)S(1)}, u32[]{:S(2)}, u32[]{:S(2)}) collective-permute-start(f32[64,128]{1,0:T(8,128)S(1)} %get-tuple-element.108), channel_id=1, source_target_pairs={{0,28},{4,8},{8,4},{12,16},{16,12},{20,24},{24,20},{28,0},{1,29},{... | collective-permute-start | bytes 98312 | tf_op jit(solution)/shard_map/ppermute | solution.py:832
  42.6 5.6 %collective-permute-start.3 = (f32[64,128]{1,0:T(8,128)S(1)}, f32[64,128]{1,0:T(8,128)S(1)}, u32[]{:S(2)}, u32[]{:S(2)}) collective-permute-start(f32[64,128]{1,0:T(8,128)S(1)} %get-tuple-element.109), channel_id=1, source_target_pairs={{0,4},{4,0},{8,12},{12,8},{16,20},{20,16},{24,28},{28,24},{1,5},{5... | collective-permute-start | bytes 98312 | tf_op jit(solution)/shard_map/ppermute | solution.py:833
  48.5 10.5 %collective-permute-start.4 = (f32[64,128]{1,0:T(8,128)S(1)}, f32[64,128]{1,0:T(8,128)S(1)}, u32[]{:S(2)}, u32[]{:S(2)}) collective-permute-start(f32[64,128]{1,0:T(8,128)S(1)} %get-tuple-element.117), channel_id=1, source_target_pairs={{0,28},{4,8},{8,4},{12,16},{16,12},{20,24},{24,20},{28,0},{1,29},{... | collective-permute-start | bytes 98312 | tf_op jit(solution)/shard_map/ppermute | solution.py:832
  52.0 7.0 %collective-permute-start.5 = (f32[64,128]{1,0:T(8,128)S(1)}, f32[64,128]{1,0:T(8,128)S(1)}, u32[]{:S(2)}, u32[]{:S(2)}) collective-permute-start(f32[64,128]{1,0:T(8,128)S(1)} %get-tuple-element.118), channel_id=1, source_target_pairs={{0,4},{4,0},{8,12},{12,8},{16,20},{20,16},{24,28},{28,24},{1,5},{5... | collective-permute-start | bytes 98312 | tf_op jit(solution)/shard_map/ppermute | solution.py:833
  59.8 16.9 %all-to-all-start.1 = ((f32[8,120,128]{2,1,0:T(8,128)}), f32[8,120,128]{2,1,0:T(8,128)S(1)}, u32[]{:S(2)}, u32[]{:S(2)}) async-start(f32[8,120,128]{2,1,0:T(8,128)} %bitcast.17), calls=%async_computation.1 | async-start | bytes 983040 | tf_op jit(solution)/shard_map/all_to_all | solution.py:901
  64.1 12.2 %collective-permute-start.6 = (f32[64,128]{1,0:T(8,128)S(1)}, f32[64,128]{1,0:T(8,128)S(1)}, u32[]{:S(2)}, u32[]{:S(2)}) collective-permute-start(f32[64,128]{1,0:T(8,128)S(1)} %get-tuple-element.127), channel_id=1, source_target_pairs={{0,28},{4,8},{8,4},{12,16},{16,12},{20,24},{24,20},{28,0},{1,29},{... | collective-permute-start | bytes 98312 | tf_op jit(solution)/shard_map/ppermute | solution.py:898
  68.8 7.5 %collective-permute-start.7 = (f32[64,128]{1,0:T(8,128)S(1)}, f32[64,128]{1,0:T(8,128)S(1)}, u32[]{:S(2)}, u32[]{:S(2)}) collective-permute-start(f32[64,128]{1,0:T(8,128)S(1)} %get-tuple-element.128), channel_id=1, source_target_pairs={{0,4},{4,0},{8,12},{12,8},{16,20},{20,16},{24,28},{28,24},{1,5},{5... | collective-permute-start | bytes 98312 | tf_op jit(solution)/shard_map/ppermute | solution.py:899
  73.2 5.5 %collective-permute-start.10 = (f32[24,128]{1,0:T(8,128)}, f32[24,128]{1,0:T(8,128)S(1)}, u32[]{:S(2)}, u32[]{:S(2)}) collective-permute-start(f32[24,128]{1,0:T(8,128)} %get-tuple-element.134), channel_id=1, source_target_pairs={{0,3},{1,2},{2,1},{3,0},{4,7},{5,6},{6,5},{7,4},{8,11},{9,10},{10,... | collective-permute-start | bytes 36872 | tf_op jit(solution)/shard_map/ppermute | solution.py:928
  73.3 5.4 %collective-permute-start.9 = (f32[24,128]{1,0:T(8,128)}, f32[24,128]{1,0:T(8,128)S(1)}, u32[]{:S(2)}, u32[]{:S(2)}) collective-permute-start(f32[24,128]{1,0:T(8,128)} %get-tuple-element.134), channel_id=1, source_target_pairs={{0,2},{1,3},{2,0},{3,1},{4,6},{5,7},{6,4},{7,5},{8,10},{9,11},{10,... | collective-permute-start | bytes 36872 | tf_op jit(solution)/shard_map/ppermute | solution.py:928
  74.8 3.9 %collective-permute-start.8 = (f32[24,128]{1,0:T(8,128)}, f32[24,128]{1,0:T(8,128)S(1)}, u32[]{:S(2)}, u32[]{:S(2)}) collective-permute-start(f32[24,128]{1,0:T(8,128)} %get-tuple-element.134), channel_id=1, source_target_pairs={{0,1},{1,0},{2,3},{3,2},{4,5},{5,4},{6,7},{7,6},{8,9},{9,8},{10,11... | collective-permute-start | bytes 36872 | tf_op jit(solution)/shard_map/ppermute | solution.py:928
where the time goes:
time: 81.3 us; the launch traced here: 80 us
  Pallas kernels  45.8 us (56%)
  starting transfers between devices  27.5 us (34%)
  waiting for transfers between devices  4.64 us (6%)
  other arithmetic  1.31 us (2%)
    pallas_call x11, Pallas kernels, call(): pl.pallas_call(kernel, name=name, out_shape=outs, in_specs=specs, out_spe...  45.8 us
    ppermute x4, starting transfers between devices, shards(): from_far = lax.ppermute(far, 'region', far_pairs)  13.4 us
    all_to_all x1, starting transfers between devices, shards(): lax.all_to_all(packed, 'region', split_axis=0, concat_axis=0, tiled=True)  7.29 us
    all_to_all x1, starting transfers between devices, shards(): lax.all_to_all(chunks, 'region', split_axis=0, concat_axis=0, tiled=True)  4.29 us
    all_to_all x1, waiting for transfers between devices, shards(): lax.all_to_all(packed, 'region', split_axis=0, concat_axis=0, tiled=True)  3.01 us
    ppermute x3, starting transfers between devices, shards(): peaks.append(lax.ppermute(peak_out, 'scen', shift))  1.92 us
  transfers between devices with their start and end apart: 13, of which 3 were waited for; matrix products, arithmetic and copies ran while one was open for 0% of the time, Pallas kernels for 43%

commit v1 on v0

--- a/solution.py
+++ b/solution.py
@@ -29,13 +29,6 @@
 def split_2(value):
     high = value.astype(BF)
     return high, (value - high.astype(F32)).astype(BF)
-
-
-def split_3(value):
-    high = value.astype(BF)
-    rest = value - high.astype(F32)
-    middle = rest.astype(BF)
-    return high, middle, (rest - middle.astype(F32)).astype(BF)
 
 
 def stacked(value):
@@ -89,7 +82,7 @@
         self.wide = (2 * self.scen, self.lanes)
         self.weights = (self.blocks, self.picks * self.width, 2 * self.padded)
         self.site_rows = (self.lanes, self.ends)
-        self.response = (self.blocks, self.ends, 2 * self.padded)
+        self.response = (self.blocks // 2, 2, self.ends, 2 * self.padded)
         self.coupling = (self.ends, 2 * self.ends)
         self.node_rows = (self.blocks, 8, self.padded)
         self.fault_cols = (2, self.scen, self.padded)
@@ -168,7 +161,7 @@
     state = jnp.concatenate([init[0], init[1]], axis=0)
     payload = jnp.concatenate([state.T, settings.T], axis=1)
     width = state.shape[0]
-    rows = sum(dot(select, part) for part in split_3(payload))
+    rows = sum(dot(select, part) for part in split_2(payload))
     for r in range(size.regions):
         chunk = rows[r * size.rows : (r + 1) * size.rows]
         out[r] = chunk[:, :width]
@@ -206,10 +199,14 @@
     down_lane = one_hot(lane == iota(square, 0).astype(F32))
     across_lane = one_hot(turned_row(lane) == iota(square, 1).astype(F32))
     zeros = jnp.zeros(square, BF)
-    for n in range(size.lanes // LANES):
-        here = jnp.asarray(n, BF)
+
+    def put(n, carry):
+        here = jnp.asarray(n, I32).astype(F32).astype(BF)
         gather(n, jnp.where(down_block == here, down_lane, zeros))
         scatter(n, jnp.where(across_block == here, across_lane, zeros))
+        return carry
+
+    lax.fori_loop(0, size.lanes // LANES, put, 0, unroll=True)
 
 
 def turned_row(row):
@@ -243,6 +240,12 @@
 def three_terms(product, rows, width):
     top, low = product[:rows], product[rows:]
     return top[:, :width] + top[:, width:] + low[:, :width]
+
+
+def corrections(size, drives, mt, pair):
+    high = folded(dot(drives, mt[pair, 0]))
+    added = high + dot(drives[: size.scen], mt[pair, 1])
+    return [(2 * pair + j, added[:, block_lanes(size, j)]) for j in range(2)]
 
 
 def apply_inverse(size, cols, x, wp, volt, vb):
@@ -285,11 +288,10 @@
     row = padded_index(nodes[...].astype(F32), size.width, size.padded)
     for c in range(0, size.ends, LANES):
         def put_gather(n, value, c=c):
-            eg[n * LANES : (n + 1) * LANES, c : c + LANES] = value
+            eg[pl.ds(pl.multiple_of(n * LANES, LANES), LANES), c : c + LANES] = value
 
         def put_scatter(n, value, c=c):
-            b, lane = n * LANES // size.padded, n * LANES % size.padded
-            es[b, c : c + LANES, lane : lane + LANES] = value
+            es[n, c : c + LANES, :] = value
 
         site_products(size, row, c, put_gather, put_scatter)
     sent.append(copies.start(eg, eg_out))
@@ -338,7 +340,9 @@
             left = jnp.concatenate([es[cols[k, b]] for k in range(size.picks)], axis=1)
             product = dot(left, jnp.concatenate(parts, axis=0))
             high, low = split_2(product[:, : size.padded] + product[:, size.padded :])
-            mt[b] = jnp.concatenate([high, low], axis=1)
+            half = pl.ds(pl.multiple_of(lax.rem(b, 2) * size.padded, LANES), size.padded)
+            mt[lax.div(b, 2), 0, :, half] = high
+            mt[lax.div(b, 2), 1, :, half] = low
             both[:, pl.ds(pl.multiple_of(b * size.padded, LANES), size.padded)] = jnp.concatenate(
                 [high, low], axis=0
             )
@@ -347,6 +351,7 @@
         lax.fori_loop(i * stage, (i + 1) * stage, turn, 0, unroll=4)
         part = pl.ds(i * stage, stage)
         sent.append(copies.start(wp.at[part], wp_out.at[part]))
+        part = pl.ds(i * stage // 2, stage // 2)
         sent.append(copies.start(mt.at[part], mt_out.at[part]))
 
     high, low = split_2(folded(dot(both[...], eg[...])))
@@ -364,11 +369,14 @@
 
 
 def for_chunks(size, count, work):
-    for c in range(size.chunks):
-        if c < 2:
-            work(c * size.chunk)
-        else:
-            pl.when(count > c)(functools.partial(work, c * size.chunk))
+    def one(c, carry):
+        work(pl.multiple_of(c * size.chunk, LANES))
+        return carry
+
+    least = min(2, size.chunks)
+    for c in range(least):
+        work(c * size.chunk)
+    lax.fori_loop(least, count, one, 0)
 
 
 def inject(size, count, pair, cs, put):
@@ -386,7 +394,7 @@
                 put(i * step + j, both[:, block_lanes(size, j)])
             return carry
 
-        lax.fori_loop(0, size.blocks // step, some_blocks, 0, unroll=True if used == least else 4)
+        lax.fori_loop(0, size.blocks // step, some_blocks, 0, unroll=True if used <= least + 1 else 1)
 
     for used in range(least, size.chunks + 1):
         if used == least:
@@ -398,7 +406,7 @@
 
 def converter_update(size, count, vb, cg, prm, filt, amps, pair):
     def update(first):
-        lanes = slice(first, first + size.chunk)
+        lanes = pl.ds(first, size.chunk)
         measured = folded(dot(vb[...], cg[:, lanes]))
         filtered = filt[:, lanes]
         filtered = filtered + prm[2:3, lanes] * (measured - filtered)
@@ -476,15 +484,16 @@
         amps[:, c : c + LANES] = turned[size.scen :]
         turned = jnp.where(valid, moved_settings[c : c + LANES, :], 0.0).T
         prm[:, c : c + LANES] = turned[:8]
-    row = padded_index(prm[3:4, :] - 1.0, size.width, size.padded)
-
     def put_products(first):
-        for c in range(first, first + size.chunk, LANES):
-            def put_gather(n, value, c=c):
-                cg[n * LANES : (n + 1) * LANES, c : c + LANES] = value
-
-            def put_scatter(n, value, c=c):
-                cs[c : c + LANES, n * LANES : (n + 1) * LANES] = value
+        row = padded_index(prm[3:4, pl.ds(first, size.chunk)] - 1.0, size.width, size.padded)
+        for c in range(0, size.chunk, LANES):
+            lanes = pl.ds(pl.multiple_of(first + c, LANES), LANES)
+
+            def put_gather(n, value, lanes=lanes):
+                cg[pl.ds(pl.multiple_of(n * LANES, LANES), LANES), lanes] = value
+
+            def put_scatter(n, value, lanes=lanes):
+                cs[lanes, pl.ds(pl.multiple_of(n * LANES, LANES), LANES)] = value
 
             site_products(size, row, c, put_gather, put_scatter)
 
@@ -525,8 +534,7 @@
     place_copy = copies.start(place_hbm, place)
     cols_copy = copies.start(cols_hbm, cols)
     drives = stacked(drive[...])
-    for b in range(size.blocks):
-        added = three_terms(dot(drives, mt[b]), size.scen, size.padded)
+    for b, added in (c for p in range(size.blocks // 2) for c in corrections(size, drives, mt, p)):
         v = volt[b] + added
         volt[b] = v
         vb[:, block_lanes(size, b)] = stacked(v)
@@ -603,21 +611,26 @@
 ):
     copies = Copies(sems)
     drive_copy = copies.start(drive_hbm, drive)
-    half = size.blocks // 2
+    pieces = 4 if size.blocks % 8 == 0 else 1
+    pairs = size.blocks // 2 // pieces
     parts = []
-    for i in range(2):
-        part = pl.ds(i * half, half)
+    for i in range(pieces):
+        part, blocks = pl.ds(i * pairs, pairs), pl.ds(2 * i * pairs, 2 * pairs)
         parts.append(
-            [copies.start(volt_hbm.at[part], volt.at[part]), copies.start(mt_hbm.at[part], mt.at[part])]
+            [
+                copies.start(volt_hbm.at[blocks], volt.at[blocks]),
+                copies.start(mt_hbm.at[part], mt.at[part]),
+            ]
         )
     peak_copy = copies.start(peak_hbm, peak)
     drive_copy.wait()
-    pair = stacked(drive[...])
-    for b in range(size.blocks):
-        if b % half == 0:
-            for copy in parts[b // half]:
+    drives = stacked(drive[...])
+    for p in range(size.blocks // 2):
+        if p % pairs == 0:
+            for copy in parts[p // pairs]:
                 copy.wait()
-        volt[b] = volt[b] + three_terms(dot(pair, mt[b]), size.scen, size.padded)
+        for b, added in corrections(size, drives, mt, p):
+            volt[b] = volt[b] + added
     peak_copy.wait()
 
     def largest(b):
@@ -642,12 +655,10 @@
     dst_copy = copies.start(dst_hbm, dst)
     newest[0] = arrived(size, far, near)
     sent = [copies.start(newest, waves_out.at[pl.ds(0, 1)])]
-    parts = jnp.concatenate(split_3(received[...].T), axis=0)
+    parts = stacked(received[...].T)
     dst_copy.wait()
     select = one_hot(iota((size.slots, size.convs), 0) == dst[...])
-    state = dot(parts, select)
-    width = 2 * size.scen
-    state = state[:width] + state[width : 2 * width] + state[2 * width :]
+    state = folded(dot(parts, select))
     state_out[0] = state[: size.scen]
     state_out[1] = state[size.scen :]
     sent.append(copies.start(state_out, state_hbm))
@@ -914,7 +925,7 @@
             vmem((scen, size.nodes), F32),
             vmem((1, size.nodes), F32),
             vmem((size.nodes // LANES, LANES), F32),
-            dma((8,)),
+            dma((12,)),
         ],
         12,
     )

time: 81.3 us -> 79.8 us (0.982); the launches traced: 80 us -> 79.4 us
  no operation moved by 1% of the time
where the time goes in v1:
time: 79.8 us; the launch traced here: 79.4 us
  Pallas kernels  45.4 us (57%)
  starting transfers between devices  27.1 us (34%)
  waiting for transfers between devices  4.75 us (6%)
  other arithmetic  1.31 us (2%)
  between operations  0.81 us (1%)
    pallas_call x11, Pallas kernels, call(): pl.pallas_call(kernel, name=name, out_shape=outs, in_specs=specs, out_spe...  45.4 us
    ppermute x4, starting transfers between devices, shards(): from_far = lax.ppermute(far, 'region', far_pairs)  13 us
    all_to_all x1, starting transfers between devices, shards(): lax.all_to_all(packed, 'region', split_axis=0, concat_axis=0, tiled=True)  7.29 us
    all_to_all x1, starting transfers between devices, shards(): lax.all_to_all(chunks, 'region', split_axis=0, concat_axis=0, tiled=True)  4.88 us
    all_to_all x1, waiting for transfers between devices, shards(): lax.all_to_all(packed, 'region', split_axis=0, concat_axis=0, tiled=True)  2.88 us
    ppermute x3, starting transfers between devices, shards(): peaks.append(lax.ppermute(peak_out, 'scen', shift))  1.92 us
  transfers between devices with their start and end apart: 13, of which 3 were waited for; matrix products, arithmetic and copies ran while one was open for 0% of the time, Pallas kernels for 43%

profile of v1, /device:TPU:0, one launch (start us, length us, event | category | flops | bytes accessed | tf_op | source)
XLA Modules:
  0.0 79.4 jit_solution(7889163121670367809)
XLA Ops:
  0.6 2.8 %pack.1 = (f32[8,120,128]{2,1,0:T(8,128)}, s32[1,384]{1,0:T(1,128)}) custom-call(s32[1,384]{1,0:T(1,128)} %bitcast.26, f32[384]{0:T(512)} %power_hbm.1, s32[384]{0:T(512)} %node_hbm.1, f32[2,384]{1,0:T(2,128)} %gains_hbm.1, f32[2,64,384]{2,1,0:T(8,128)} %init_hbm.1), custom_call_target="tpu_custom_call" | custom-call | tf_op jit(solution)/shard_map/pack/pallas_call | solution.py:682
  3.4 7.3 %all-to-all-start = ((f32[8,120,128]{2,1,0:T(8,128)}), f32[8,120,128]{2,1,0:T(8,128)S(1)}, u32[]{:S(2)}, u32[]{:S(2)}) async-start(f32[8,120,128]{2,1,0:T(8,128)} %get-tuple-element.70), calls=%async_computation | async-start | bytes 983040 | tf_op jit(solution)/shard_map/all_to_all | solution.py:729
  10.7 10.9 %prep.1 = (bf16[32,480,256]{2,1,0:T(8,128)(2,1)}, bf16[4096,256]{1,0:T(8,128)(2,1)}, bf16[16,2,256,256]{3,2,1,0:T(8,128)(2,1)}, bf16[256,512]{1,0:T(8,128)(2,1)}...) custom-call(s32[5,32]{1,0:T(8,128)} %bitcast.18, ...), custom_call_target="tpu_custom_call" | custom-call | tf_op jit(solution)/shard_map/prep/pallas_call | solution.py:682
  21.6 2.9 %all-to-all-done = f32[8,120,128]{2,1,0:T(8,128)S(1)} async-done(((f32[8,120,128]{2,1,0:T(8,128)}), f32[8,120,128]{2,1,0:T(8,128)S(1)}, u32[]{:S(2)}, u32[]{:S(2)}) %all-to-all-start) | async-done | bytes 491552 | tf_op jit(solution)/shard_map/all_to_all | solution.py:729
  24.5 7.0 %start.1 = (bf16[32,480,256]{2,1,0:T(8,128)(2,1)S(1)}, bf16[4096,256]{1,0:T(8,128)(2,1)S(1)}, bf16[16,2,256,256]{3,2,1,0:T(8,128)(2,1)S(1)}, bf16[256,512]{1,0:T...) custom-call(s32[5,32]{1,0:T(8,128)} %bitcast.19, ...), custom_call_target="tpu_custom_call" | custom-call | tf_op jit(solution)/shard_map/start/pallas_call | solution.py:682
  31.5 2.4 %collective-permute-start = (f32[64,128]{1,0:T(8,128)S(1)}, f32[64,128]{1,0:T(8,128)S(1)}, u32[]{:S(2)}, u32[]{:S(2)}) collective-permute-start(f32[64,128]{1,0:T(8,128)S(1)} %get-tuple-element.99), channel_id=1, source_target_pairs={{0,28},{4,8},{8,4},{12,16},{16,12},{20,24},{24,20},{28,0},{1,29},{... | collective-permute-start | bytes 98312 | tf_op jit(solution)/shard_map/ppermute | solution.py:843
  33.9 0.0 collective-permute-start.1
  33.9 5.6 %middle.3 = (f32[32,64,128]{2,1,0:T(8,128)S(1)}, f32[64,1024]{1,0:T(8,128)S(1)}, f32[64,1024]{1,0:T(8,128)S(1)}, f32[32,64,128]{2,1,0:T(8,128)S(1)}, f32[32,8,128]{2,1,0:T(8,128)S(1)}, /*index=5*/f32[64,256]{1,0:T(8,128)S(1)}) custom-call(s32[5,32]{1,0:T(8,128)} %bitcast.20, ...), custom_call_target="tpu_custom_call", output_to_operand_aliasing={{0}: (11, {}), {1}: (12, {}), {2}: (13, {}), {3}: (14, {}),... | custom-call | tf_op jit(solution)/shard_map/middle/pallas_call | solution.py:682
  39.5 0.0 collective-permute-done.refs_0_.refs_2_.refs_4_
  39.5 0.2 launch.3
  39.7 3.0 %collective-permute-start.2 = (f32[64,128]{1,0:T(8,128)S(1)}, f32[64,128]{1,0:T(8,128)S(1)}, u32[]{:S(2)}, u32[]{:S(2)}) collective-permute-start(f32[64,128]{1,0:T(8,128)S(1)} %get-tuple-element.108), channel_id=1, source_target_pairs={{0,28},{4,8},{8,4},{12,16},{16,12},{20,24},{24,20},{28,0},{1,29},{... | collective-permute-start | bytes 98312 | tf_op jit(solution)/shard_map/ppermute | solution.py:843
  42.7 5.8 %middle.4 = (f32[32,64,128]{2,1,0:T(8,128)S(1)}, f32[64,1024]{1,0:T(8,128)S(1)}, f32[64,1024]{1,0:T(8,128)S(1)}, f32[32,64,128]{2,1,0:T(8,128)S(1)}, f32[32,8,128]{2,1,0:T(8,128)S(1)}, /*index=5*/f32[64,256]{1,0:T(8,128)S(1)}) custom-call(s32[5,32]{1,0:T(8,128)} %bitcast.21, ...), custom_call_target="tpu_custom_call", output_to_operand_aliasing={{0}: (11, {}), {1}: (12, {}), {2}: (13, {}), {3}: (14, {}),... | custom-call | tf_op jit(solution)/shard_map/middle/pallas_call | solution.py:682
  48.5 0.0 collective-permute-done.3.refs_1_.refs_3_
  48.5 0.2 launch.4
  48.7 2.8 %collective-permute-start.4 = (f32[64,128]{1,0:T(8,128)S(1)}, f32[64,128]{1,0:T(8,128)S(1)}, u32[]{:S(2)}, u32[]{:S(2)}) collective-permute-start(f32[64,128]{1,0:T(8,128)S(1)} %get-tuple-element.117), channel_id=1, source_target_pairs={{0,28},{4,8},{8,4},{12,16},{16,12},{20,24},{24,20},{28,0},{1,29},{... | collective-permute-start | bytes 98312 | tf_op jit(solution)/shard_map/ppermute | solution.py:843
  51.5 0.0 collective-permute-start.5
  51.6 6.1 %middle.5 = (f32[32,64,128]{2,1,0:T(8,128)S(1)}, f32[64,1024]{1,0:T(8,128)S(1)}, f32[64,1024]{1,0:T(8,128)S(1)}, f32[32,64,128]{2,1,0:T(8,128)S(1)}, f32[32,8,12...) custom-call(s32[5,32]{1,0:T(8,128)} %bitcast.22, ...), custom_call_target="tpu_custom_call", output_to_operand_aliasing={{0}: (11, {}), {1}: (12, {}), {2}: (13, {}), {3}: (14, {}),... | custom-call | tf_op jit(solution)/shard_map/middle/pallas_call | solution.py:682
  57.7 0.0 collective-permute-done.5.refs_1_
  57.7 0.8 %launch.5 = (f32[64,256]{1,0:T(8,128)}, f32[64,128]{1,0:T(8,128)S(1)}, f32[64,128]{1,0:T(8,128)S(1)}, f32[960,128]{1,0:T(8,128)}, f32[8,64,256]{2,1,0:T(8,128)}) custom-call(f32[64,256]{1,0:T(8,128)S(1)} %get-tuple-element.116.at_ends, bf16[256,512]{1,0:T(8,128)(2,1)S(1)} %get-tuple-element.96.kk, ...), custom_call_target="tpu_custom_call", output_to_operand_aliasing={{3}: (10, {})} | custom-call | tf_op jit(solution)/shard_map/launch/pallas_call | solution.py:682
  58.5 4.9 %all-to-all-start.1 = ((f32[8,120,128]{2,1,0:T(8,128)}), f32[8,120,128]{2,1,0:T(8,128)S(1)}, u32[]{:S(2)}, u32[]{:S(2)}) async-start(f32[8,120,128]{2,1,0:T(8,128)} %bitcast.17), calls=%async_computation.1 | async-start | bytes 983040 | tf_op jit(solution)/shard_map/all_to_all | solution.py:912
  63.4 4.7 %collective-permute-start.6 = (f32[64,128]{1,0:T(8,128)S(1)}, f32[64,128]{1,0:T(8,128)S(1)}, u32[]{:S(2)}, u32[]{:S(2)}) collective-permute-start(f32[64,128]{1,0:T(8,128)S(1)} %get-tuple-element.127), channel_id=1, source_target_pairs={{0,28},{4,8},{8,4},{12,16},{16,12},{20,24},{24,20},{28,0},{1,29},{... | collective-permute-start | bytes 98312 | tf_op jit(solution)/shard_map/ppermute | solution.py:909
  68.1 0.0 collective-permute-start.7
  68.1 4.2 %final.1 = (f32[64,3072]{1,0:T(8,128)}, f32[24,128]{1,0:T(8,128)}) custom-call(f32[64,256]{1,0:T(8,128)} %get-tuple-element.120.drive_hbm, f32[32,64,128]{2,1,0:T(8,128)} %get-tuple-element.121.volt_hbm, bf16[16,2,256,256]{3,2,1,0:T(8,128)(2,1)} %get-tuple-element.73.mt_hbm, f32[32,8,128]{2,1,0:T(8,128)} %get-tuple-element.122.peak_hbm), custom_call_target="tpu_custom_call" | custom-call | tf_op jit(solution)/shard_map/final/pallas_call | solution.py:682
  72.3 0.1 collective-permute-start.10
  72.4 1.6 %collective-permute-start.9 = (f32[24,128]{1,0:T(8,128)}, f32[24,128]{1,0:T(8,128)S(1)}, u32[]{:S(2)}, u32[]{:S(2)}) collective-permute-start(f32[24,128]{1,0:T(8,128)} %get-tuple-element.134), channel_id=1, source_target_pairs={{0,2},{1,3},{2,0},{3,1},{4,6},{5,7},{6,4},{7,5},{8,10},{9,11},{10,... | collective-permute-start | bytes 36872 | tf_op jit(solution)/shard_map/ppermute | solution.py:939
  73.9 0.3 collective-permute-start.8
  74.2 1.5 %collective-permute-done.6.far = f32[64,128]{1,0:T(8,128)S(1)} collective-permute-done((f32[64,128]{1,0:T(8,128)S(1)}, f32[64,128]{1,0:T(8,128)S(1)}, u32[]{:S(2)}, u32[]{:S(2)}) %collective-permute-start.6) | collective-permute-done | bytes 32800 | tf_op jit(solution)/shard_map/ppermute | solution.py:909
  75.7 0.0 collective-permute-done.7.near
  75.7 0.4 all-to-all-done.1
  76.1 1.9 %end.1 = (f32[2,64,384]{2,1,0:T(8,128)}, f32[8,64,256]{2,1,0:T(8,128)}) custom-call(s32[1,384]{1,0:T(1,128)} %get-tuple-element.125.dst_hbm, f32[960,128]{1,0:T(8,128)S(1)} %bitcast.15, f32[64,128]{1,0:T(8,128)S(1)} %collective-permute-done.6.far, f32[64,128]{1,0:T(8,128)S(1)} %collective-permute-done.7.near, ...), custom_call_target="tpu_custom_call", output_to_operand_aliasing={{1}: (4, {})} | custom-call | tf_op jit(solution)/shard_map/end/pallas_call | solution.py:682
  78.1 0.0 collective-permute-done.8
  78.1 1.3 %maximum_bitcast_fusion = f32[3072]{0:T(1024)} fusion(f32[24,128]{1,0:T(8,128)S(1)} %collective-permute-done.10, f32[24,128]{1,0:T(8,128)S(1)} %collective-permute-done.9, f32[24,128]{1,0:T(8,128)} %get-tuple-element.134, f32[24,128]{1,0:T(8,128)S(1)} %collective-permute-done.8), kind=kLoop, calls=%fused_computation | loop fusion | flops 9216 | bytes 61440 | tf_op jit(solution)/shard_map/reshape | solution.py:960
  (6 shorter events, 0.0 us)
Async XLA Ops:
  3.4 21.1 %all-to-all-start = ((f32[8,120,128]{2,1,0:T(8,128)}), f32[8,120,128]{2,1,0:T(8,128)S(1)}, u32[]{:S(2)}, u32[]{:S(2)}) async-start(f32[8,120,128]{2,1,0:T(8,128)} %get-tuple-element.70), calls=%async_computation | async-start | bytes 983040 | tf_op jit(solution)/shard_map/all_to_all | solution.py:729
  31.5 8.0 %collective-permute-start = (f32[64,128]{1,0:T(8,128)S(1)}, f32[64,128]{1,0:T(8,128)S(1)}, u32[]{:S(2)}, u32[]{:S(2)}) collective-permute-start(f32[64,128]{1,0:T(8,128)S(1)} %get-tuple-element.99), channel_id=1, source_target_pairs={{0,28},{4,8},{8,4},{12,16},{16,12},{20,24},{24,20},{28,0},{1,29},{... | collective-permute-start | bytes 98312 | tf_op jit(solution)/shard_map/ppermute | solution.py:843
  33.9 5.6 %collective-permute-start.1 = (f32[64,128]{1,0:T(8,128)S(1)}, f32[64,128]{1,0:T(8,128)S(1)}, u32[]{:S(2)}, u32[]{:S(2)}) collective-permute-start(f32[64,128]{1,0:T(8,128)S(1)} %get-tuple-element.100), channel_id=1, source_target_pairs={{0,4},{4,0},{8,12},{12,8},{16,20},{20,16},{24,28},{28,24},{1,5},{5... | collective-permute-start | bytes 98312 | tf_op jit(solution)/shard_map/ppermute | solution.py:844
  39.7 8.8 %collective-permute-start.2 = (f32[64,128]{1,0:T(8,128)S(1)}, f32[64,128]{1,0:T(8,128)S(1)}, u32[]{:S(2)}, u32[]{:S(2)}) collective-permute-start(f32[64,128]{1,0:T(8,128)S(1)} %get-tuple-element.108), channel_id=1, source_target_pairs={{0,28},{4,8},{8,4},{12,16},{16,12},{20,24},{24,20},{28,0},{1,29},{... | collective-permute-start | bytes 98312 | tf_op jit(solution)/shard_map/ppermute | solution.py:843
  42.7 5.8 %collective-permute-start.3 = (f32[64,128]{1,0:T(8,128)S(1)}, f32[64,128]{1,0:T(8,128)S(1)}, u32[]{:S(2)}, u32[]{:S(2)}) collective-permute-start(f32[64,128]{1,0:T(8,128)S(1)} %get-tuple-element.109), channel_id=1, source_target_pairs={{0,4},{4,0},{8,12},{12,8},{16,20},{20,16},{24,28},{28,24},{1,5},{5... | collective-permute-start | bytes 98312 | tf_op jit(solution)/shard_map/ppermute | solution.py:844
  48.7 9.0 %collective-permute-start.4 = (f32[64,128]{1,0:T(8,128)S(1)}, f32[64,128]{1,0:T(8,128)S(1)}, u32[]{:S(2)}, u32[]{:S(2)}) collective-permute-start(f32[64,128]{1,0:T(8,128)S(1)} %get-tuple-element.117), channel_id=1, source_target_pairs={{0,28},{4,8},{8,4},{12,16},{16,12},{20,24},{24,20},{28,0},{1,29},{... | collective-permute-start | bytes 98312 | tf_op jit(solution)/shard_map/ppermute | solution.py:843
  51.5 6.1 %collective-permute-start.5 = (f32[64,128]{1,0:T(8,128)S(1)}, f32[64,128]{1,0:T(8,128)S(1)}, u32[]{:S(2)}, u32[]{:S(2)}) collective-permute-start(f32[64,128]{1,0:T(8,128)S(1)} %get-tuple-element.118), channel_id=1, source_target_pairs={{0,4},{4,0},{8,12},{12,8},{16,20},{20,16},{24,28},{28,24},{1,5},{5... | collective-permute-start | bytes 98312 | tf_op jit(solution)/shard_map/ppermute | solution.py:844
  58.5 17.5 %all-to-all-start.1 = ((f32[8,120,128]{2,1,0:T(8,128)}), f32[8,120,128]{2,1,0:T(8,128)S(1)}, u32[]{:S(2)}, u32[]{:S(2)}) async-start(f32[8,120,128]{2,1,0:T(8,128)} %bitcast.17), calls=%async_computation.1 | async-start | bytes 983040 | tf_op jit(solution)/shard_map/all_to_all | solution.py:912
  63.4 12.3 %collective-permute-start.6 = (f32[64,128]{1,0:T(8,128)S(1)}, f32[64,128]{1,0:T(8,128)S(1)}, u32[]{:S(2)}, u32[]{:S(2)}) collective-permute-start(f32[64,128]{1,0:T(8,128)S(1)} %get-tuple-element.127), channel_id=1, source_target_pairs={{0,28},{4,8},{8,4},{12,16},{16,12},{20,24},{24,20},{28,0},{1,29},{... | collective-permute-start | bytes 98312 | tf_op jit(solution)/shard_map/ppermute | solution.py:909
  68.1 7.6 %collective-permute-start.7 = (f32[64,128]{1,0:T(8,128)S(1)}, f32[64,128]{1,0:T(8,128)S(1)}, u32[]{:S(2)}, u32[]{:S(2)}) collective-permute-start(f32[64,128]{1,0:T(8,128)S(1)} %get-tuple-element.128), channel_id=1, source_target_pairs={{0,4},{4,0},{8,12},{12,8},{16,20},{20,16},{24,28},{28,24},{1,5},{5... | collective-permute-start | bytes 98312 | tf_op jit(solution)/shard_map/ppermute | solution.py:910
  72.3 5.7 %collective-permute-start.10 = (f32[24,128]{1,0:T(8,128)}, f32[24,128]{1,0:T(8,128)S(1)}, u32[]{:S(2)}, u32[]{:S(2)}) collective-permute-start(f32[24,128]{1,0:T(8,128)} %get-tuple-element.134), channel_id=1, source_target_pairs={{0,3},{1,2},{2,1},{3,0},{4,7},{5,6},{6,5},{7,4},{8,11},{9,10},{10,... | collective-permute-start | bytes 36872 | tf_op jit(solution)/shard_map/ppermute | solution.py:939
  72.4 5.7 %collective-permute-start.9 = (f32[24,128]{1,0:T(8,128)}, f32[24,128]{1,0:T(8,128)S(1)}, u32[]{:S(2)}, u32[]{:S(2)}) collective-permute-start(f32[24,128]{1,0:T(8,128)} %get-tuple-element.134), channel_id=1, source_target_pairs={{0,2},{1,3},{2,0},{3,1},{4,6},{5,7},{6,4},{7,5},{8,10},{9,11},{10,... | collective-permute-start | bytes 36872 | tf_op jit(solution)/shard_map/ppermute | solution.py:939
  73.9 4.1 %collective-permute-start.8 = (f32[24,128]{1,0:T(8,128)}, f32[24,128]{1,0:T(8,128)S(1)}, u32[]{:S(2)}, u32[]{:S(2)}) collective-permute-start(f32[24,128]{1,0:T(8,128)} %get-tuple-element.134), channel_id=1, source_target_pairs={{0,1},{1,0},{2,3},{3,2},{4,5},{5,4},{6,7},{7,6},{8,9},{9,8},{10,11... | collective-permute-start | bytes 36872 | tf_op jit(solution)/shard_map/ppermute | solution.py:939

commit v2 on v1

--- a/solution.py
+++ b/solution.py
@@ -523,16 +523,21 @@
 def middle_kernel(
     size, last,
     cols_hbm, place_hbm, drive, wp, eg, mt, node_rows, fault_cols, cg, cs, prm,
-    branch_in, filt_in, amps_in, volt_in, peak_in,
-    branch, filt, amps, volt, peak, at_ends, *refs,
+    branch_in, filt_in, amps_in, volt_in, peak_in, *refs,
 ):
     if last:
-        back_hbm, branch_hbm, volt_hbm, peak_hbm, branch_out, moved, back = *refs[:4], *refs[-3:]
-        refs = refs[4:-3]
+        dst_hbm, refs = refs[0], refs[1:]
+    branch, filt, amps, volt, peak, at_ends, *refs = refs
+    if last:
+        back_hbm, branch_hbm, volt_hbm, peak_hbm, *refs = refs
+        branch_out, moved, back, dst = refs[-4:]
+        refs = refs[:-4]
     cols, place, x, vb, pair, sems = refs
     copies = Copies(sems)
     place_copy = copies.start(place_hbm, place)
     cols_copy = copies.start(cols_hbm, cols)
+    if last:
+        dst_copy = copies.start(dst_hbm, dst)
     drives = stacked(drive[...])
     for b, added in (c for p in range(size.blocks // 2) for c in corrections(size, drives, mt, p)):
         v = volt[b] + added
@@ -563,6 +568,9 @@
         moved[size.slot_lanes :, :] = jnp.zeros((size.rows, 2 * size.scen), F32)
         for r in range(size.regions):
             back[r * size.rows : (r + 1) * size.rows, :] = moved[pl.ds(place[r], size.rows), :]
+        dst_copy.wait()
+        for row, lanes in own_rows(size):
+            back[pl.ds(row, 1), :] = dst[:, lanes].astype(F32)
         unpad_blocks(size, lambda b: branch[b], branch_out)
         sent = [
             copies.start(back, back_hbm),
@@ -576,6 +584,12 @@
     if last:
         for copy in sent:
             copy.wait()
+
+
+def own_rows(size):
+    width = 2 * size.scen
+    first = lax.axis_index("region") * size.rows + size.capacity
+    return [(first + i, slice(i * width, (i + 1) * width)) for i in range(size.convs // width)]
 
 
 def launch_kernel(size, done, last, at_ends, kk, ends, waves, *refs):
@@ -648,16 +662,14 @@
 
 
 def end_kernel(
-    size, dst_hbm, received, far, near, waves_in, state_hbm, waves_out,
-    dst, newest, state_out, sems,
+    size, received, far, near, waves_in, state_hbm, waves_out, newest, state_out, sems
 ):
     copies = Copies(sems)
-    dst_copy = copies.start(dst_hbm, dst)
     newest[0] = arrived(size, far, near)
     sent = [copies.start(newest, waves_out.at[pl.ds(0, 1)])]
     parts = stacked(received[...].T)
-    dst_copy.wait()
-    select = one_hot(iota((size.slots, size.convs), 0) == dst[...])
+    dst = jnp.concatenate([received[pl.ds(row, 1), :] for row, _ in own_rows(size)], axis=1)
+    select = one_hot(iota((size.slots, size.convs), 0) == dst.astype(I32))
     state = folded(dot(parts, select))
     state_out[0] = state[: size.scen]
     state_out[1] = state[size.scen :]
@@ -851,7 +863,7 @@
             vmem(size.drive, F32),
         ]
         specs = [VMEM] * len(outs)
-        scratch = [cols_scratch, place_scratch, x_scratch, wide_scratch, pair_scratch, dma((6,))]
+        scratch = [cols_scratch, place_scratch, x_scratch, wide_scratch, pair_scratch, dma((7,))]
         if last:
             outs += [
                 hbm((size.slots, 2 * scen), F32),
@@ -864,6 +876,7 @@
                 vmem((scen, size.nodes), F32),
                 moved_scratch,
                 vmem((size.slots, 2 * scen), F32),
+                vmem(dst.shape, I32),
             ]
         result = call(
             functools.partial(middle_kernel, size, last),
@@ -873,8 +886,9 @@
             in_hbm(cols, place)
             + in_vmem(
                 drive, wp, eg, mt, node_rows, fault_cols, cg, cs, prm, branch, filt, amps, volt, peak
-            ),
-            [HBM] * 2 + [VMEM] * 14,
+            )
+            + (in_hbm(dst) if last else []),
+            [HBM] * 2 + [VMEM] * 14 + ([HBM] if last else []),
             scratch,
             12,
             {11: 0, 12: 1, 13: 2, 14: 3, 15: 4},
@@ -943,16 +957,15 @@
         "end",
         [hbm(conv_init.shape, F32), hbm(wave_init.shape, F32)],
         [HBM] * 2,
-        in_hbm(dst) + in_vmem(returned, from_far, from_near) + in_hbm(waves_out),
-        [HBM, VMEM, VMEM, VMEM, HBM],
+        in_vmem(returned, from_far, from_near) + in_hbm(waves_out),
+        [VMEM, VMEM, VMEM, HBM],
         [
-            vmem(dst.shape, I32),
             vmem((1, *size.drive), F32),
             vmem(conv_init.shape, F32),
-            dma((3,)),
+            dma((2,)),
         ],
         16,
-        {4: 1},
+        {3: 1},
     )
     envelope, conv_state = lax.optimization_barrier((peak_out, conv_state))
     for peak in peaks:

time: 79.8 us -> 79.2 us (level)
  starting transfers between devices: 27.1 us -> 24 us
  Pallas kernels: 45.4 us -> 48.3 us
    pallas_call x11, Pallas kernels: 45.4 us -> 48.3 us  [call(): pl.pallas_call(kernel, name=name, out_shape=outs, in_specs=specs, out_spe...]
    ppermute x4, starting transfers between devices: 13 us -> 10.3 us  [shards(): from_far = lax.ppermute(far, 'region', far_pairs)]
  transfers between devices with their start and end apart: 13 -> 13, of which waited for: 3 -> 3; matrix products, arithmetic and copies ran while one was open for 0% -> 0% of each run, Pallas kernels for 43% -> 46%
where the time goes in v2:
time: 79.2 us; the launch traced here: 78.8 us
  Pallas kernels  48.3 us (61%)
  starting transfers between devices  24 us (30%)
  waiting for transfers between devices  4.36 us (6%)
  other arithmetic  1.31 us (2%)
  between operations  0.8 us (1%)
    pallas_call x11, Pallas kernels, call(): pl.pallas_call(kernel, name=name, out_shape=outs, in_specs=specs, out_spe...  48.3 us
    ppermute x4, starting transfers between devices, shards(): from_far = lax.ppermute(far, 'region', far_pairs)  10.3 us
    all_to_all x1, starting transfers between devices, shards(): lax.all_to_all(packed, 'region', split_axis=0, concat_axis=0, tiled=True)  7.29 us
    all_to_all x1, starting transfers between devices, shards(): lax.all_to_all(chunks, 'region', split_axis=0, concat_axis=0, tiled=True)  4.48 us
    all_to_all x1, waiting for transfers between devices, shards(): lax.all_to_all(packed, 'region', split_axis=0, concat_axis=0, tiled=True)  2.88 us
    ppermute x3, starting transfers between devices, shards(): peaks.append(lax.ppermute(peak_out, 'scen', shift))  1.92 us
  transfers between devices with their start and end apart: 13, of which 3 were waited for; matrix products, arithmetic and copies ran while one was open for 0% of the time, Pallas kernels for 46%

profile of v2, /device:TPU:0, one launch (start us, length us, event | category | flops | bytes accessed | tf_op | source)
XLA Modules:
  0.0 78.8 jit_solution(14312409160088992203)
XLA Ops:
  0.6 2.8 %pack.1 = (f32[8,120,128]{2,1,0:T(8,128)}, s32[1,384]{1,0:T(1,128)}) custom-call(s32[1,384]{1,0:T(1,128)} %bitcast.26, f32[384]{0:T(512)} %power_hbm.1, s32[384]{0:T(512)} %node_hbm.1, f32[2,384]{1,0:T(2,128)} %gains_hbm.1, f32[2,64,384]{2,1,0:T(8,128)} %init_hbm.1), custom_call_target="tpu_custom_call" | custom-call | tf_op jit(solution)/shard_map/pack/pallas_call | solution.py:694
  3.4 7.3 %all-to-all-start = ((f32[8,120,128]{2,1,0:T(8,128)}), f32[8,120,128]{2,1,0:T(8,128)S(1)}, u32[]{:S(2)}, u32[]{:S(2)}) async-start(f32[8,120,128]{2,1,0:T(8,128)} %get-tuple-element.70), calls=%async_computation | async-start | bytes 983040 | tf_op jit(solution)/shard_map/all_to_all | solution.py:741
  10.7 10.9 %prep.1 = (bf16[32,480,256]{2,1,0:T(8,128)(2,1)}, bf16[4096,256]{1,0:T(8,128)(2,1)}, bf16[16,2,256,256]{3,2,1,0:T(8,128)(2,1)}, bf16[256,512]{1,0:T(8,128)(2,1)}...) custom-call(s32[5,32]{1,0:T(8,128)} %bitcast.18, ...), custom_call_target="tpu_custom_call" | custom-call | tf_op jit(solution)/shard_map/prep/pallas_call | solution.py:694
  21.6 2.9 %all-to-all-done = f32[8,120,128]{2,1,0:T(8,128)S(1)} async-done(((f32[8,120,128]{2,1,0:T(8,128)}), f32[8,120,128]{2,1,0:T(8,128)S(1)}, u32[]{:S(2)}, u32[]{:S(2)}) %all-to-all-start) | async-done | bytes 491552 | tf_op jit(solution)/shard_map/all_to_all | solution.py:741
  24.5 8.4 %start.1 = (bf16[32,480,256]{2,1,0:T(8,128)(2,1)S(1)}, bf16[4096,256]{1,0:T(8,128)(2,1)S(1)}, bf16[16,2,256,256]{3,2,1,0:T(8,128)(2,1)S(1)}, bf16[256,512]{1,0:T...) custom-call(s32[5,32]{1,0:T(8,128)} %bitcast.19, ...), custom_call_target="tpu_custom_call" | custom-call | tf_op jit(solution)/shard_map/start/pallas_call | solution.py:694
  32.9 1.0 %collective-permute-start = (f32[64,128]{1,0:T(8,128)S(1)}, f32[64,128]{1,0:T(8,128)S(1)}, u32[]{:S(2)}, u32[]{:S(2)}) collective-permute-start(f32[64,128]{1,0:T(8,128)S(1)} %get-tuple-element.99), channel_id=1, source_target_pairs={{0,28},{4,8},{8,4},{12,16},{16,12},{20,24},{24,20},{28,0},{1,29},{... | collective-permute-start | bytes 98312 | tf_op jit(solution)/shard_map/ppermute | solution.py:855
  33.9 0.0 collective-permute-start.1
  33.9 6.3 %middle.3 = (f32[32,64,128]{2,1,0:T(8,128)S(1)}, f32[64,1024]{1,0:T(8,128)S(1)}, f32[64,1024]{1,0:T(8,128)S(1)}, f32[32,64,128]{2,1,0:T(8,128)S(1)}, f32[32,8,128]{2,1,0:T(8,128)S(1)}, /*index=5*/f32[64,256]{1,0:T(8,128)S(1)}) custom-call(s32[5,32]{1,0:T(8,128)} %bitcast.20, ...), custom_call_target="tpu_custom_call", output_to_operand_aliasing={{0}: (11, {}), {1}: (12, {}), {2}: (13, {}), {3}: (14, {}),... | custom-call | tf_op jit(solution)/shard_map/middle/pallas_call | solution.py:694
  40.2 0.0 collective-permute-done.refs_0_.refs_2_.refs_4_
  40.2 0.0 collective-permute-done.1.refs_1_.refs_3_.refs_5_
  40.2 0.2 launch.3
  40.4 3.1 %collective-permute-start.2 = (f32[64,128]{1,0:T(8,128)S(1)}, f32[64,128]{1,0:T(8,128)S(1)}, u32[]{:S(2)}, u32[]{:S(2)}) collective-permute-start(f32[64,128]{1,0:T(8,128)S(1)} %get-tuple-element.108), channel_id=1, source_target_pairs={{0,28},{4,8},{8,4},{12,16},{16,12},{20,24},{24,20},{28,0},{1,29},{... | collective-permute-start | bytes 98312 | tf_op jit(solution)/shard_map/ppermute | solution.py:855
  43.5 0.0 collective-permute-start.3
  43.5 6.5 %middle.4 = (f32[32,64,128]{2,1,0:T(8,128)S(1)}, f32[64,1024]{1,0:T(8,128)S(1)}, f32[64,1024]{1,0:T(8,128)S(1)}, f32[32,64,128]{2,1,0:T(8,128)S(1)}, f32[32,8,128]{2,1,0:T(8,128)S(1)}, /*index=5*/f32[64,256]{1,0:T(8,128)S(1)}) custom-call(s32[5,32]{1,0:T(8,128)} %bitcast.21, ...), custom_call_target="tpu_custom_call", output_to_operand_aliasing={{0}: (11, {}), {1}: (12, {}), {2}: (13, {}), {3}: (14, {}),... | custom-call | tf_op jit(solution)/shard_map/middle/pallas_call | solution.py:694
  50.1 0.0 collective-permute-done.2.refs_0_.refs_2_
  50.1 0.0 collective-permute-done.3.refs_1_.refs_3_
  50.1 0.2 launch.4
  50.3 1.4 %collective-permute-start.4 = (f32[64,128]{1,0:T(8,128)S(1)}, f32[64,128]{1,0:T(8,128)S(1)}, u32[]{:S(2)}, u32[]{:S(2)}) collective-permute-start(f32[64,128]{1,0:T(8,128)S(1)} %get-tuple-element.118), channel_id=1, source_target_pairs={{0,28},{4,8},{8,4},{12,16},{16,12},{20,24},{24,20},{28,0},{1,29},{... | collective-permute-start | bytes 98312 | tf_op jit(solution)/shard_map/ppermute | solution.py:855
  51.7 6.9 %middle.5 = (f32[32,64,128]{2,1,0:T(8,128)S(1)}, f32[64,1024]{1,0:T(8,128)S(1)}, f32[64,1024]{1,0:T(8,128)S(1)}, f32[32,64,128]{2,1,0:T(8,128)S(1)}, f32[32,8,12...) custom-call(s32[5,32]{1,0:T(8,128)} %bitcast.22, ...), custom_call_target="tpu_custom_call", output_to_operand_aliasing={{0}: (11, {}), {1}: (12, {}), {2}: (13, {}), {3}: (14, {}),... | custom-call | tf_op jit(solution)/shard_map/middle/pallas_call | solution.py:694
  58.6 0.8 %launch.5 = (f32[64,256]{1,0:T(8,128)}, f32[64,128]{1,0:T(8,128)S(1)}, f32[64,128]{1,0:T(8,128)S(1)}, f32[960,128]{1,0:T(8,128)}, f32[8,64,256]{2,1,0:T(8,128)}) custom-call(f32[64,256]{1,0:T(8,128)S(1)} %get-tuple-element.117.at_ends, bf16[256,512]{1,0:T(8,128)(2,1)S(1)} %get-tuple-element.96.kk, ...), custom_call_target="tpu_custom_call", output_to_operand_aliasing={{3}: (10, {})} | custom-call | tf_op jit(solution)/shard_map/launch/pallas_call | solution.py:694
  59.5 4.5 %all-to-all-start.1 = ((f32[8,120,128]{2,1,0:T(8,128)}), f32[8,120,128]{2,1,0:T(8,128)S(1)}, u32[]{:S(2)}, u32[]{:S(2)}) async-start(f32[8,120,128]{2,1,0:T(8,128)} %bitcast.17), calls=%async_computation.1 | async-start | bytes 983040 | tf_op jit(solution)/shard_map/all_to_all | solution.py:926
  64.0 4.7 %collective-permute-start.6 = (f32[64,128]{1,0:T(8,128)S(1)}, f32[64,128]{1,0:T(8,128)S(1)}, u32[]{:S(2)}, u32[]{:S(2)}) collective-permute-start(f32[64,128]{1,0:T(8,128)S(1)} %get-tuple-element.127), channel_id=1, source_target_pairs={{0,28},{4,8},{8,4},{12,16},{16,12},{20,24},{24,20},{28,0},{1,29},{... | collective-permute-start | bytes 98312 | tf_op jit(solution)/shard_map/ppermute | solution.py:923
  68.7 4.2 %final.1 = (f32[64,3072]{1,0:T(8,128)}, f32[24,128]{1,0:T(8,128)}) custom-call(f32[64,256]{1,0:T(8,128)} %get-tuple-element.121.drive_hbm, f32[32,64,128]{2,1,0:T(8,128)} %get-tuple-element.122.volt_hbm, bf16[16,2,256,256]{3,2,1,0:T(8,128)(2,1)} %get-tuple-element.73.mt_hbm, f32[32,8,128]{2,1,0:T(8,128)} %get-tuple-element.123.peak_hbm), custom_call_target="tpu_custom_call" | custom-call | tf_op jit(solution)/shard_map/final/pallas_call | solution.py:694
  72.9 0.1 collective-permute-start.10
  72.9 1.6 %collective-permute-start.9 = (f32[24,128]{1,0:T(8,128)}, f32[24,128]{1,0:T(8,128)S(1)}, u32[]{:S(2)}, u32[]{:S(2)}) collective-permute-start(f32[24,128]{1,0:T(8,128)} %get-tuple-element.134), channel_id=1, source_target_pairs={{0,2},{1,3},{2,0},{3,1},{4,6},{5,7},{6,4},{7,5},{8,10},{9,11},{10,... | collective-permute-start | bytes 36872 | tf_op jit(solution)/shard_map/ppermute | solution.py:953
  74.5 0.3 collective-permute-start.8
  74.8 1.1 %collective-permute-done.6.far = f32[64,128]{1,0:T(8,128)S(1)} collective-permute-done((f32[64,128]{1,0:T(8,128)S(1)}, f32[64,128]{1,0:T(8,128)S(1)}, u32[]{:S(2)}, u32[]{:S(2)}) %collective-permute-start.6) | collective-permute-done | bytes 32800 | tf_op jit(solution)/shard_map/ppermute | solution.py:923
  75.9 0.0 collective-permute-done.7.near
  75.9 0.3 all-to-all-done.1
  76.2 1.2 %end.1 = (f32[2,64,384]{2,1,0:T(8,128)}, f32[8,64,256]{2,1,0:T(8,128)}) custom-call(f32[960,128]{1,0:T(8,128)S(1)} %bitcast.15, f32[64,128]{1,0:T(8,128)S(1)} %collective-permute-done.6.far, f32[64,128]{1,0:T(8,128)S(1)} %collective-permute-done.7.near, f32[8,64,256]{2,1,0:T(8,128)} %get-tuple-element.129.waves_in), custom_call_target="tpu_custom_call", output_to_operand_aliasing={{1}: (3, {})} | custom-call | tf_op jit(solution)/shard_map/end/pallas_call | solution.py:694
  77.4 0.0 collective-permute-done.9
  77.5 1.3 %maximum_bitcast_fusion = f32[3072]{0:T(1024)} fusion(f32[24,128]{1,0:T(8,128)S(1)} %collective-permute-done.10, f32[24,128]{1,0:T(8,128)S(1)} %collective-permute-done.9, f32[24,128]{1,0:T(8,128)} %get-tuple-element.134, f32[24,128]{1,0:T(8,128)S(1)} %collective-permute-done.8), kind=kLoop, calls=%fused_computation | loop fusion | flops 9216 | bytes 61440 | tf_op jit(solution)/shard_map/reshape | solution.py:973
  (6 shorter events, 0.0 us)
Async XLA Ops:
  3.4 21.1 %all-to-all-start = ((f32[8,120,128]{2,1,0:T(8,128)}), f32[8,120,128]{2,1,0:T(8,128)S(1)}, u32[]{:S(2)}, u32[]{:S(2)}) async-start(f32[8,120,128]{2,1,0:T(8,128)} %get-tuple-element.70), calls=%async_computation | async-start | bytes 983040 | tf_op jit(solution)/shard_map/all_to_all | solution.py:741
  32.9 7.3 %collective-permute-start = (f32[64,128]{1,0:T(8,128)S(1)}, f32[64,128]{1,0:T(8,128)S(1)}, u32[]{:S(2)}, u32[]{:S(2)}) collective-permute-start(f32[64,128]{1,0:T(8,128)S(1)} %get-tuple-element.99), channel_id=1, source_target_pairs={{0,28},{4,8},{8,4},{12,16},{16,12},{20,24},{24,20},{28,0},{1,29},{... | collective-permute-start | bytes 98312 | tf_op jit(solution)/shard_map/ppermute | solution.py:855
  33.9 6.3 %collective-permute-start.1 = (f32[64,128]{1,0:T(8,128)S(1)}, f32[64,128]{1,0:T(8,128)S(1)}, u32[]{:S(2)}, u32[]{:S(2)}) collective-permute-start(f32[64,128]{1,0:T(8,128)S(1)} %get-tuple-element.100), channel_id=1, source_target_pairs={{0,4},{4,0},{8,12},{12,8},{16,20},{20,16},{24,28},{28,24},{1,5},{5... | collective-permute-start | bytes 98312 | tf_op jit(solution)/shard_map/ppermute | solution.py:856
  40.4 9.6 %collective-permute-start.2 = (f32[64,128]{1,0:T(8,128)S(1)}, f32[64,128]{1,0:T(8,128)S(1)}, u32[]{:S(2)}, u32[]{:S(2)}) collective-permute-start(f32[64,128]{1,0:T(8,128)S(1)} %get-tuple-element.108), channel_id=1, source_target_pairs={{0,28},{4,8},{8,4},{12,16},{16,12},{20,24},{24,20},{28,0},{1,29},{... | collective-permute-start | bytes 98312 | tf_op jit(solution)/shard_map/ppermute | solution.py:855
  43.5 6.5 %collective-permute-start.3 = (f32[64,128]{1,0:T(8,128)S(1)}, f32[64,128]{1,0:T(8,128)S(1)}, u32[]{:S(2)}, u32[]{:S(2)}) collective-permute-start(f32[64,128]{1,0:T(8,128)S(1)} %get-tuple-element.109), channel_id=1, source_target_pairs={{0,4},{4,0},{8,12},{12,8},{16,20},{20,16},{24,28},{28,24},{1,5},{5... | collective-permute-start | bytes 98312 | tf_op jit(solution)/shard_map/ppermute | solution.py:856
  50.3 8.3 %collective-permute-start.4 = (f32[64,128]{1,0:T(8,128)S(1)}, f32[64,128]{1,0:T(8,128)S(1)}, u32[]{:S(2)}, u32[]{:S(2)}) collective-permute-start(f32[64,128]{1,0:T(8,128)S(1)} %get-tuple-element.118), channel_id=1, source_target_pairs={{0,28},{4,8},{8,4},{12,16},{16,12},{20,24},{24,20},{28,0},{1,29},{... | collective-permute-start | bytes 98312 | tf_op jit(solution)/shard_map/ppermute | solution.py:855
  51.7 6.9 %collective-permute-start.5 = (f32[64,128]{1,0:T(8,128)S(1)}, f32[64,128]{1,0:T(8,128)S(1)}, u32[]{:S(2)}, u32[]{:S(2)}) collective-permute-start(f32[64,128]{1,0:T(8,128)S(1)} %get-tuple-element.119), channel_id=1, source_target_pairs={{0,4},{4,0},{8,12},{12,8},{16,20},{20,16},{24,28},{28,24},{1,5},{5... | collective-permute-start | bytes 98312 | tf_op jit(solution)/shard_map/ppermute | solution.py:856
  59.5 16.7 %all-to-all-start.1 = ((f32[8,120,128]{2,1,0:T(8,128)}), f32[8,120,128]{2,1,0:T(8,128)S(1)}, u32[]{:S(2)}, u32[]{:S(2)}) async-start(f32[8,120,128]{2,1,0:T(8,128)} %bitcast.17), calls=%async_computation.1 | async-start | bytes 983040 | tf_op jit(solution)/shard_map/all_to_all | solution.py:926
  64.0 11.9 %collective-permute-start.6 = (f32[64,128]{1,0:T(8,128)S(1)}, f32[64,128]{1,0:T(8,128)S(1)}, u32[]{:S(2)}, u32[]{:S(2)}) collective-permute-start(f32[64,128]{1,0:T(8,128)S(1)} %get-tuple-element.127), channel_id=1, source_target_pairs={{0,28},{4,8},{8,4},{12,16},{16,12},{20,24},{24,20},{28,0},{1,29},{... | collective-permute-start | bytes 98312 | tf_op jit(solution)/shard_map/ppermute | solution.py:923
  68.7 7.2 %collective-permute-start.7 = (f32[64,128]{1,0:T(8,128)S(1)}, f32[64,128]{1,0:T(8,128)S(1)}, u32[]{:S(2)}, u32[]{:S(2)}) collective-permute-start(f32[64,128]{1,0:T(8,128)S(1)} %get-tuple-element.128), channel_id=1, source_target_pairs={{0,4},{4,0},{8,12},{12,8},{16,20},{20,16},{24,28},{28,24},{1,5},{5... | collective-permute-start | bytes 98312 | tf_op jit(solution)/shard_map/ppermute | solution.py:924
  72.9 4.6 %collective-permute-start.10 = (f32[24,128]{1,0:T(8,128)}, f32[24,128]{1,0:T(8,128)S(1)}, u32[]{:S(2)}, u32[]{:S(2)}) collective-permute-start(f32[24,128]{1,0:T(8,128)} %get-tuple-element.134), channel_id=1, source_target_pairs={{0,3},{1,2},{2,1},{3,0},{4,7},{5,6},{6,5},{7,4},{8,11},{9,10},{10,... | collective-permute-start | bytes 36872 | tf_op jit(solution)/shard_map/ppermute | solution.py:953
  72.9 4.5 %collective-permute-start.9 = (f32[24,128]{1,0:T(8,128)}, f32[24,128]{1,0:T(8,128)S(1)}, u32[]{:S(2)}, u32[]{:S(2)}) collective-permute-start(f32[24,128]{1,0:T(8,128)} %get-tuple-element.134), channel_id=1, source_target_pairs={{0,2},{1,3},{2,0},{3,1},{4,6},{5,7},{6,4},{7,5},{8,10},{9,11},{10,... | collective-permute-start | bytes 36872 | tf_op jit(solution)/shard_map/ppermute | solution.py:953
  74.5 3.0 %collective-permute-start.8 = (f32[24,128]{1,0:T(8,128)}, f32[24,128]{1,0:T(8,128)S(1)}, u32[]{:S(2)}, u32[]{:S(2)}) collective-permute-start(f32[24,128]{1,0:T(8,128)} %get-tuple-element.134), channel_id=1, source_target_pairs={{0,1},{1,0},{2,3},{3,2},{4,5},{5,4},{6,7},{7,6},{8,9},{9,8},{10,11... | collective-permute-start | bytes 36872 | tf_op jit(solution)/shard_map/ppermute | solution.py:953

commit v3 on v2

--- a/solution.py
+++ b/solution.py
@@ -168,7 +168,7 @@
         filler = jnp.zeros((LANES - size.rows, LANES), F32)
         turned = jnp.concatenate([chunk[:, width:], filler], axis=0).T
         out[r, size.capacity : size.capacity + 4, :] = turned[:4]
-    sent.append(copies.start(out, out_hbm))
+        sent.append(copies.start(out.at[r], out_hbm.at[r]))
     for copy in sent:
         copy.wait()
 
@@ -244,7 +244,7 @@
 
 def corrections(size, drives, mt, pair):
     high = folded(dot(drives, mt[pair, 0]))
-    added = high + dot(drives[: size.scen], mt[pair, 1])
+    added = high + dot(drives, mt[pair, 1])[: size.scen]
     return [(2 * pair + j, added[:, block_lanes(size, j)]) for j in range(2)]
 
 
@@ -734,7 +734,7 @@
             vmem(conv_init.shape, F32),
             vmem(chunk, F32),
             vmem((1, size.convs), I32),
-            dma((8,)),
+            dma((8 + regions,)),
         ],
         16,
     )

time: 79.2 us -> 78.1 us (0.986)
  Pallas kernels: 48.3 us -> 44.4 us
  starting transfers between devices: 24 us -> 26.7 us
    pallas_call x11, Pallas kernels: 48.3 us -> 44.4 us  [call(): pl.pallas_call(kernel, name=name, out_shape=outs, in_specs=specs, out_spe...]
    ppermute x4, starting transfers between devices: 10.3 us -> 12.6 us  [shards(): from_far = lax.ppermute(far, 'region', far_pairs)]
  transfers between devices with their start and end apart: 13 -> 13, of which waited for: 3 -> 3; matrix products, arithmetic and copies ran while one was open for 0% -> 0% of each run, Pallas kernels for 46% -> 43%
where the time goes in v3:
time: 78.1 us; the launch traced here: 77.8 us
  Pallas kernels  44.4 us (57%)
  starting transfers between devices  26.7 us (34%)
  waiting for transfers between devices  4.56 us (6%)
  other arithmetic  1.31 us (2%)
  between operations  0.8 us (1%)
    pallas_call x11, Pallas kernels, call(): pl.pallas_call(kernel, name=name, out_shape=outs, in_specs=specs, out_spe...  44.4 us
    ppermute x4, starting transfers between devices, shards(): from_far = lax.ppermute(far, 'region', far_pairs)  12.6 us
    all_to_all x1, starting transfers between devices, shards(): lax.all_to_all(packed, 'region', split_axis=0, concat_axis=0, tiled=True)  7.29 us
    all_to_all x1, starting transfers between devices, shards(): lax.all_to_all(chunks, 'region', split_axis=0, concat_axis=0, tiled=True)  4.5 us
    all_to_all x1, waiting for transfers between devices, shards(): lax.all_to_all(packed, 'region', split_axis=0, concat_axis=0, tiled=True)  2.88 us
    ppermute x3, starting transfers between devices, shards(): peaks.append(lax.ppermute(peak_out, 'scen', shift))  1.92 us
  transfers between devices with their start and end apart: 13, of which 3 were waited for; matrix products, arithmetic and copies ran while one was open for 0% of the time, Pallas kernels for 43%

profile of v3, /device:TPU:0, one launch (start us, length us, event | category | flops | bytes accessed | tf_op | source)
XLA Modules:
  0.0 77.8 jit_solution(14989996926050482868)
XLA Ops:
  0.6 2.8 %pack.1 = (f32[8,120,128]{2,1,0:T(8,128)}, s32[1,384]{1,0:T(1,128)}) custom-call(s32[1,384]{1,0:T(1,128)} %bitcast.26, f32[384]{0:T(512)} %power_hbm.1, s32[384]{0:T(512)} %node_hbm.1, f32[2,384]{1,0:T(2,128)} %gains_hbm.1, f32[2,64,384]{2,1,0:T(8,128)} %init_hbm.1), custom_call_target="tpu_custom_call" | custom-call | tf_op jit(solution)/shard_map/pack/pallas_call | solution.py:694
  3.4 7.3 %all-to-all-start = ((f32[8,120,128]{2,1,0:T(8,128)}), f32[8,120,128]{2,1,0:T(8,128)S(1)}, u32[]{:S(2)}, u32[]{:S(2)}) async-start(f32[8,120,128]{2,1,0:T(8,128)} %get-tuple-element.70), calls=%async_computation | async-start | bytes 983040 | tf_op jit(solution)/shard_map/all_to_all | solution.py:741
  10.7 10.9 %prep.1 = (bf16[32,480,256]{2,1,0:T(8,128)(2,1)}, bf16[4096,256]{1,0:T(8,128)(2,1)}, bf16[16,2,256,256]{3,2,1,0:T(8,128)(2,1)}, bf16[256,512]{1,0:T(8,128)(2,1)}...) custom-call(s32[5,32]{1,0:T(8,128)} %bitcast.18, ...), custom_call_target="tpu_custom_call" | custom-call | tf_op jit(solution)/shard_map/prep/pallas_call | solution.py:694
  21.6 2.9 %all-to-all-done = f32[8,120,128]{2,1,0:T(8,128)S(1)} async-done(((f32[8,120,128]{2,1,0:T(8,128)}), f32[8,120,128]{2,1,0:T(8,128)S(1)}, u32[]{:S(2)}, u32[]{:S(2)}) %all-to-all-start) | async-done | bytes 491552 | tf_op jit(solution)/shard_map/all_to_all | solution.py:741
  24.5 7.0 %start.1 = (bf16[32,480,256]{2,1,0:T(8,128)(2,1)S(1)}, bf16[4096,256]{1,0:T(8,128)(2,1)S(1)}, bf16[16,2,256,256]{3,2,1,0:T(8,128)(2,1)S(1)}, bf16[256,512]{1,0:T...) custom-call(s32[5,32]{1,0:T(8,128)} %bitcast.19, ...), custom_call_target="tpu_custom_call" | custom-call | tf_op jit(solution)/shard_map/start/pallas_call | solution.py:694
  31.5 2.4 %collective-permute-start = (f32[64,128]{1,0:T(8,128)S(1)}, f32[64,128]{1,0:T(8,128)S(1)}, u32[]{:S(2)}, u32[]{:S(2)}) collective-permute-start(f32[64,128]{1,0:T(8,128)S(1)} %get-tuple-element.99), channel_id=1, source_target_pairs={{0,28},{4,8},{8,4},{12,16},{16,12},{20,24},{24,20},{28,0},{1,29},{... | collective-permute-start | bytes 98312 | tf_op jit(solution)/shard_map/ppermute | solution.py:855
  33.9 0.0 collective-permute-start.1
  33.9 5.4 %middle.3 = (f32[32,64,128]{2,1,0:T(8,128)S(1)}, f32[64,1024]{1,0:T(8,128)S(1)}, f32[64,1024]{1,0:T(8,128)S(1)}, f32[32,64,128]{2,1,0:T(8,128)S(1)}, f32[32,8,128]{2,1,0:T(8,128)S(1)}, /*index=5*/f32[64,256]{1,0:T(8,128)S(1)}) custom-call(s32[5,32]{1,0:T(8,128)} %bitcast.20, ...), custom_call_target="tpu_custom_call", output_to_operand_aliasing={{0}: (11, {}), {1}: (12, {}), {2}: (13, {}), {3}: (14, {}),... | custom-call | tf_op jit(solution)/shard_map/middle/pallas_call | solution.py:694
  39.4 0.0 collective-permute-done.refs_0_.refs_2_.refs_4_
  39.4 0.0 collective-permute-done.1.refs_1_.refs_3_.refs_5_
  39.4 0.2 launch.3
  39.6 3.0 %collective-permute-start.2 = (f32[64,128]{1,0:T(8,128)S(1)}, f32[64,128]{1,0:T(8,128)S(1)}, u32[]{:S(2)}, u32[]{:S(2)}) collective-permute-start(f32[64,128]{1,0:T(8,128)S(1)} %get-tuple-element.108), channel_id=1, source_target_pairs={{0,28},{4,8},{8,4},{12,16},{16,12},{20,24},{24,20},{28,0},{1,29},{... | collective-permute-start | bytes 98312 | tf_op jit(solution)/shard_map/ppermute | solution.py:855
  42.6 5.7 %middle.4 = (f32[32,64,128]{2,1,0:T(8,128)S(1)}, f32[64,1024]{1,0:T(8,128)S(1)}, f32[64,1024]{1,0:T(8,128)S(1)}, f32[32,64,128]{2,1,0:T(8,128)S(1)}, f32[32,8,128]{2,1,0:T(8,128)S(1)}, /*index=5*/f32[64,256]{1,0:T(8,128)S(1)}) custom-call(s32[5,32]{1,0:T(8,128)} %bitcast.21, ...), custom_call_target="tpu_custom_call", output_to_operand_aliasing={{0}: (11, {}), {1}: (12, {}), {2}: (13, {}), {3}: (14, {}),... | custom-call | tf_op jit(solution)/shard_map/middle/pallas_call | solution.py:694
  48.3 0.0 collective-permute-done.2.refs_0_.refs_2_
  48.3 0.0 collective-permute-done.3.refs_1_.refs_3_
  48.3 0.2 launch.4
  48.5 2.5 %collective-permute-start.4 = (f32[64,128]{1,0:T(8,128)S(1)}, f32[64,128]{1,0:T(8,128)S(1)}, u32[]{:S(2)}, u32[]{:S(2)}) collective-permute-start(f32[64,128]{1,0:T(8,128)S(1)} %get-tuple-element.118), channel_id=1, source_target_pairs={{0,28},{4,8},{8,4},{12,16},{16,12},{20,24},{24,20},{28,0},{1,29},{... | collective-permute-start | bytes 98312 | tf_op jit(solution)/shard_map/ppermute | solution.py:855
  51.0 0.4 collective-permute-start.5
  51.4 6.0 %middle.5 = (f32[32,64,128]{2,1,0:T(8,128)S(1)}, f32[64,1024]{1,0:T(8,128)S(1)}, f32[64,1024]{1,0:T(8,128)S(1)}, f32[32,64,128]{2,1,0:T(8,128)S(1)}, f32[32,8,12...) custom-call(s32[5,32]{1,0:T(8,128)} %bitcast.22, ...), custom_call_target="tpu_custom_call", output_to_operand_aliasing={{0}: (11, {}), {1}: (12, {}), {2}: (13, {}), {3}: (14, {}),... | custom-call | tf_op jit(solution)/shard_map/middle/pallas_call | solution.py:694
  57.4 0.0 collective-permute-done.4.refs_0_
  57.4 0.8 %launch.5 = (f32[64,256]{1,0:T(8,128)}, f32[64,128]{1,0:T(8,128)S(1)}, f32[64,128]{1,0:T(8,128)S(1)}, f32[960,128]{1,0:T(8,128)}, f32[8,64,256]{2,1,0:T(8,128)}) custom-call(f32[64,256]{1,0:T(8,128)S(1)} %get-tuple-element.117.at_ends, bf16[256,512]{1,0:T(8,128)(2,1)S(1)} %get-tuple-element.96.kk, ...), custom_call_target="tpu_custom_call", output_to_operand_aliasing={{3}: (10, {})} | custom-call | tf_op jit(solution)/shard_map/launch/pallas_call | solution.py:694
  58.3 4.5 %all-to-all-start.1 = ((f32[8,120,128]{2,1,0:T(8,128)}), f32[8,120,128]{2,1,0:T(8,128)S(1)}, u32[]{:S(2)}, u32[]{:S(2)}) async-start(f32[8,120,128]{2,1,0:T(8,128)} %bitcast.17), calls=%async_computation.1 | async-start | bytes 983040 | tf_op jit(solution)/shard_map/all_to_all | solution.py:926
  62.8 4.7 %collective-permute-start.6 = (f32[64,128]{1,0:T(8,128)S(1)}, f32[64,128]{1,0:T(8,128)S(1)}, u32[]{:S(2)}, u32[]{:S(2)}) collective-permute-start(f32[64,128]{1,0:T(8,128)S(1)} %get-tuple-element.127), channel_id=1, source_target_pairs={{0,28},{4,8},{8,4},{12,16},{16,12},{20,24},{24,20},{28,0},{1,29},{... | collective-permute-start | bytes 98312 | tf_op jit(solution)/shard_map/ppermute | solution.py:923
  67.5 4.2 %final.1 = (f32[64,3072]{1,0:T(8,128)}, f32[24,128]{1,0:T(8,128)}) custom-call(f32[64,256]{1,0:T(8,128)} %get-tuple-element.121.drive_hbm, f32[32,64,128]{2,1,0:T(8,128)} %get-tuple-element.122.volt_hbm, bf16[16,2,256,256]{3,2,1,0:T(8,128)(2,1)} %get-tuple-element.73.mt_hbm, f32[32,8,128]{2,1,0:T(8,128)} %get-tuple-element.123.peak_hbm), custom_call_target="tpu_custom_call" | custom-call | tf_op jit(solution)/shard_map/final/pallas_call | solution.py:694
  71.7 0.1 collective-permute-start.10
  71.7 1.6 %collective-permute-start.9 = (f32[24,128]{1,0:T(8,128)}, f32[24,128]{1,0:T(8,128)S(1)}, u32[]{:S(2)}, u32[]{:S(2)}) collective-permute-start(f32[24,128]{1,0:T(8,128)} %get-tuple-element.134), channel_id=1, source_target_pairs={{0,2},{1,3},{2,0},{3,1},{4,6},{5,7},{6,4},{7,5},{8,10},{9,11},{10,... | collective-permute-start | bytes 36872 | tf_op jit(solution)/shard_map/ppermute | solution.py:953
  73.3 0.3 collective-permute-start.8
  73.6 1.3 %collective-permute-done.6.far = f32[64,128]{1,0:T(8,128)S(1)} collective-permute-done((f32[64,128]{1,0:T(8,128)S(1)}, f32[64,128]{1,0:T(8,128)S(1)}, u32[]{:S(2)}, u32[]{:S(2)}) %collective-permute-start.6) | collective-permute-done | bytes 32800 | tf_op jit(solution)/shard_map/ppermute | solution.py:923
  74.9 0.4 all-to-all-done.1
  75.2 1.2 %end.1 = (f32[2,64,384]{2,1,0:T(8,128)}, f32[8,64,256]{2,1,0:T(8,128)}) custom-call(f32[960,128]{1,0:T(8,128)S(1)} %bitcast.15, f32[64,128]{1,0:T(8,128)S(1)} %collective-permute-done.6.far, f32[64,128]{1,0:T(8,128)S(1)} %collective-permute-done.7.near, f32[8,64,256]{2,1,0:T(8,128)} %get-tuple-element.129.waves_in), custom_call_target="tpu_custom_call", output_to_operand_aliasing={{1}: (3, {})} | custom-call | tf_op jit(solution)/shard_map/end/pallas_call | solution.py:694
  76.5 0.0 collective-permute-done.8
  76.5 1.3 %maximum_bitcast_fusion = f32[3072]{0:T(1024)} fusion(f32[24,128]{1,0:T(8,128)S(1)} %collective-permute-done.10, f32[24,128]{1,0:T(8,128)S(1)} %collective-permute-done.9, f32[24,128]{1,0:T(8,128)} %get-tuple-element.134, f32[24,128]{1,0:T(8,128)S(1)} %collective-permute-done.8), kind=kLoop, calls=%fused_computation | loop fusion | flops 9216 | bytes 61440 | tf_op jit(solution)/shard_map/reshape | solution.py:973
  (6 shorter events, 0.0 us)
Async XLA Ops:
  3.4 21.1 %all-to-all-start = ((f32[8,120,128]{2,1,0:T(8,128)}), f32[8,120,128]{2,1,0:T(8,128)S(1)}, u32[]{:S(2)}, u32[]{:S(2)}) async-start(f32[8,120,128]{2,1,0:T(8,128)} %get-tuple-element.70), calls=%async_computation | async-start | bytes 983040 | tf_op jit(solution)/shard_map/all_to_all | solution.py:741
  31.5 7.9 %collective-permute-start = (f32[64,128]{1,0:T(8,128)S(1)}, f32[64,128]{1,0:T(8,128)S(1)}, u32[]{:S(2)}, u32[]{:S(2)}) collective-permute-start(f32[64,128]{1,0:T(8,128)S(1)} %get-tuple-element.99), channel_id=1, source_target_pairs={{0,28},{4,8},{8,4},{12,16},{16,12},{20,24},{24,20},{28,0},{1,29},{... | collective-permute-start | bytes 98312 | tf_op jit(solution)/shard_map/ppermute | solution.py:855
  33.9 5.5 %collective-permute-start.1 = (f32[64,128]{1,0:T(8,128)S(1)}, f32[64,128]{1,0:T(8,128)S(1)}, u32[]{:S(2)}, u32[]{:S(2)}) collective-permute-start(f32[64,128]{1,0:T(8,128)S(1)} %get-tuple-element.100), channel_id=1, source_target_pairs={{0,4},{4,0},{8,12},{12,8},{16,20},{20,16},{24,28},{28,24},{1,5},{5... | collective-permute-start | bytes 98312 | tf_op jit(solution)/shard_map/ppermute | solution.py:856
  39.6 8.7 %collective-permute-start.2 = (f32[64,128]{1,0:T(8,128)S(1)}, f32[64,128]{1,0:T(8,128)S(1)}, u32[]{:S(2)}, u32[]{:S(2)}) collective-permute-start(f32[64,128]{1,0:T(8,128)S(1)} %get-tuple-element.108), channel_id=1, source_target_pairs={{0,28},{4,8},{8,4},{12,16},{16,12},{20,24},{24,20},{28,0},{1,29},{... | collective-permute-start | bytes 98312 | tf_op jit(solution)/shard_map/ppermute | solution.py:855
  42.6 5.7 %collective-permute-start.3 = (f32[64,128]{1,0:T(8,128)S(1)}, f32[64,128]{1,0:T(8,128)S(1)}, u32[]{:S(2)}, u32[]{:S(2)}) collective-permute-start(f32[64,128]{1,0:T(8,128)S(1)} %get-tuple-element.109), channel_id=1, source_target_pairs={{0,4},{4,0},{8,12},{12,8},{16,20},{20,16},{24,28},{28,24},{1,5},{5... | collective-permute-start | bytes 98312 | tf_op jit(solution)/shard_map/ppermute | solution.py:856
  48.5 8.9 %collective-permute-start.4 = (f32[64,128]{1,0:T(8,128)S(1)}, f32[64,128]{1,0:T(8,128)S(1)}, u32[]{:S(2)}, u32[]{:S(2)}) collective-permute-start(f32[64,128]{1,0:T(8,128)S(1)} %get-tuple-element.118), channel_id=1, source_target_pairs={{0,28},{4,8},{8,4},{12,16},{16,12},{20,24},{24,20},{28,0},{1,29},{... | collective-permute-start | bytes 98312 | tf_op jit(solution)/shard_map/ppermute | solution.py:855
  51.0 6.5 %collective-permute-start.5 = (f32[64,128]{1,0:T(8,128)S(1)}, f32[64,128]{1,0:T(8,128)S(1)}, u32[]{:S(2)}, u32[]{:S(2)}) collective-permute-start(f32[64,128]{1,0:T(8,128)S(1)} %get-tuple-element.119), channel_id=1, source_target_pairs={{0,4},{4,0},{8,12},{12,8},{16,20},{20,16},{24,28},{28,24},{1,5},{5... | collective-permute-start | bytes 98312 | tf_op jit(solution)/shard_map/ppermute | solution.py:856
  58.3 17.0 %all-to-all-start.1 = ((f32[8,120,128]{2,1,0:T(8,128)}), f32[8,120,128]{2,1,0:T(8,128)S(1)}, u32[]{:S(2)}, u32[]{:S(2)}) async-start(f32[8,120,128]{2,1,0:T(8,128)} %bitcast.17), calls=%async_computation.1 | async-start | bytes 983040 | tf_op jit(solution)/shard_map/all_to_all | solution.py:926
  62.8 12.1 %collective-permute-start.6 = (f32[64,128]{1,0:T(8,128)S(1)}, f32[64,128]{1,0:T(8,128)S(1)}, u32[]{:S(2)}, u32[]{:S(2)}) collective-permute-start(f32[64,128]{1,0:T(8,128)S(1)} %get-tuple-element.127), channel_id=1, source_target_pairs={{0,28},{4,8},{8,4},{12,16},{16,12},{20,24},{24,20},{28,0},{1,29},{... | collective-permute-start | bytes 98312 | tf_op jit(solution)/shard_map/ppermute | solution.py:923
  67.5 7.4 %collective-permute-start.7 = (f32[64,128]{1,0:T(8,128)S(1)}, f32[64,128]{1,0:T(8,128)S(1)}, u32[]{:S(2)}, u32[]{:S(2)}) collective-permute-start(f32[64,128]{1,0:T(8,128)S(1)} %get-tuple-element.128), channel_id=1, source_target_pairs={{0,4},{4,0},{8,12},{12,8},{16,20},{20,16},{24,28},{28,24},{1,5},{5... | collective-permute-start | bytes 98312 | tf_op jit(solution)/shard_map/ppermute | solution.py:924
  71.7 4.8 %collective-permute-start.10 = (f32[24,128]{1,0:T(8,128)}, f32[24,128]{1,0:T(8,128)S(1)}, u32[]{:S(2)}, u32[]{:S(2)}) collective-permute-start(f32[24,128]{1,0:T(8,128)} %get-tuple-element.134), channel_id=1, source_target_pairs={{0,3},{1,2},{2,1},{3,0},{4,7},{5,6},{6,5},{7,4},{8,11},{9,10},{10,... | collective-permute-start | bytes 36872 | tf_op jit(solution)/shard_map/ppermute | solution.py:953
  71.7 4.7 %collective-permute-start.9 = (f32[24,128]{1,0:T(8,128)}, f32[24,128]{1,0:T(8,128)S(1)}, u32[]{:S(2)}, u32[]{:S(2)}) collective-permute-start(f32[24,128]{1,0:T(8,128)} %get-tuple-element.134), channel_id=1, source_target_pairs={{0,2},{1,3},{2,0},{3,1},{4,6},{5,7},{6,4},{7,5},{8,10},{9,11},{10,... | collective-permute-start | bytes 36872 | tf_op jit(solution)/shard_map/ppermute | solution.py:953
  73.3 3.1 %collective-permute-start.8 = (f32[24,128]{1,0:T(8,128)}, f32[24,128]{1,0:T(8,128)S(1)}, u32[]{:S(2)}, u32[]{:S(2)}) collective-permute-start(f32[24,128]{1,0:T(8,128)} %get-tuple-element.134), channel_id=1, source_target_pairs={{0,1},{1,0},{2,3},{3,2},{4,5},{5,4},{6,7},{7,6},{8,9},{9,8},{10,11... | collective-permute-start | bytes 36872 | tf_op jit(solution)/shard_map/ppermute | solution.py:953
